TPU v7x, 32 devices: a whole 2x2x4 slice. The times are simulated.
32 devices in a mesh: rep: 2 (over y), ad: 4 (over z), tp: 4 (over x, core).
Axes of the slice: x: 2, y: 2, z: 4, core: 2. Of those that a mesh axis runs over, the one named last changes fastest.
Arguments:
- activations: bfloat16 [4, 1024, 8192], P(None, ('rep', 'ad'), 'tp'), parts along dimension 1, may hold values from -6 to 6
- adapter_ids: int32 [4, 1024], P(None, ('rep', 'ad')), parts along dimension 1, may hold values from 0 to 127, as said below
- owner_slots: int32 [256], P('rep'), parts along dimension 0, may hold values from 0 to 127, as said below
- base_weight: bfloat16 [8192, 8192], P(None, 'tp'), may hold values from -0.0625 to 0.0625
- shrink_weight: bfloat16 [256, 8192, 64], P(('rep', 'ad'), 'tp'), parts along dimension 0, may hold values from -0.0625 to 0.0625
- expand_weight: bfloat16 [256, 64, 8192], P(('rep', 'ad'), None, 'tp'), parts along dimension 0, may hold values from -0.75 to 0.75
Outputs:
- result: bfloat16 [4, 1024, 8192], P(None, ('rep', 'ad'), 'tp'), parts along dimension 1
There are 2 independent parts, one for each index of `rep`. A program takes and returns all parts, laid end to end along the dimension named above; an argument that names none is the same for every part. Nothing has to cross between parts.
Inputs may be any that keep to these rules, and one draw needn't show every extreme that they name: `owner_slots`: A permutation: each entry of the stacked adapter arrays belongs to exactly one adapter. `adapter_ids`: of the 128 rows that one index of ad holds in one step, at most 64 have a slot in the block of entries stored by one index of ad (slot // 32); some index of ad reaches 64 in every step.
All inputs are finite; a program needn't handle non-finite values.
Results may differ from a plain program's by a relative error of at most 0.005.
Values may be sent and summed in bfloat16 or wider, within the bound.
A program may use at most 192 MiB of HBM per device.

v0:
```python
import jax
import jax.numpy as jnp
from jax import lax
from jax.sharding import PartitionSpec as P


def owner_blocks(rows_in, select_in, shrink_weight, expand_weight):
    lead = rows_in.shape[:3]
    width_local = rows_in.shape[3]
    adp_dev = shrink_weight.shape[0]
    total = rows_in.shape[0] * rows_in.shape[1] * rows_in.shape[2]
    block_count = total // 16 + adp_dev
    flat_rows = rows_in.reshape(total, width_local)
    flat_select = select_in.reshape(total, adp_dev)
    marked = flat_select > 0
    valid = jnp.any(marked, axis=-1)
    which = jnp.sum(jnp.where(marked, jnp.arange(adp_dev, dtype=jnp.int32), 0), axis=-1)
    sort_key = jnp.where(valid, which, adp_dev)
    order = jnp.argsort(sort_key, stable=True)
    sorted_key = sort_key[order]
    counts = jnp.sum(marked.astype(jnp.int32), axis=0)
    padded = (counts + 15) // 16 * 16
    block_start = jnp.cumsum(padded) - padded
    first_sorted = jnp.cumsum(counts) - counts
    safe_key = jnp.minimum(sorted_key, adp_dev - 1)
    rank_sorted = jnp.arange(total, dtype=jnp.int32) - first_sorted[safe_key]
    limit = block_count * 16
    pos_sorted = jnp.where(sorted_key < adp_dev, block_start[safe_key] + rank_sorted, limit)
    position = jnp.zeros((total,), jnp.int32).at[order].set(pos_sorted)
    buffer_rows = (
        jnp.zeros((limit, width_local), rows_in.dtype).at[position].set(flat_rows, mode="drop")
    )
    block_rows = buffer_rows.reshape(block_count, 16, width_local)
    block_first = jnp.arange(block_count, dtype=jnp.int32) * 16
    block_end = block_start + padded
    block_adapter = jnp.sum((block_end[None, :] <= block_first[:, None]).astype(jnp.int32), axis=-1)
    block_adapter = jnp.minimum(block_adapter, adp_dev - 1)
    shrink_blocks = shrink_weight[block_adapter]
    partial_value = jnp.einsum(
        "bjf,bfe->bje", block_rows, shrink_blocks, preferred_element_type=jnp.float32
    )
    low_rank = lax.psum(partial_value, "tp").astype(jnp.bfloat16)
    expand_blocks = expand_weight[block_adapter]
    block_delta = jnp.einsum(
        "bje,bef->bjf", low_rank, expand_blocks, preferred_element_type=jnp.float32
    ).astype(jnp.bfloat16)
    delta_flat = block_delta.reshape(limit, width_local)
    fetched = delta_flat[jnp.minimum(position, limit - 1)]
    fetched = jnp.where(valid[:, None], fetched, jnp.zeros_like(fetched))
    return fetched.reshape(lead + (width_local,))


def apply_steps(step_acts, step_ids, owner_slots, base_weight, shrink_weight, expand_weight):
    step_count, row_count, width_local = step_acts.shape
    adp_dev = shrink_weight.shape[0]
    adapters = owner_slots.shape[0]
    groups = lax.axis_size("ad")
    capacity = row_count // 2
    flat_rows = step_acts.reshape(step_count * row_count, width_local)
    base_out = jnp.dot(
        lax.all_gather(flat_rows, "tp", axis=1, tiled=True),
        base_weight,
        preferred_element_type=jnp.float32,
    )
    matches = step_ids[..., None] == jnp.arange(adapters, dtype=jnp.int32)
    slot_index = jnp.sum(jnp.where(matches, owner_slots, 0), axis=-1)
    owner_group = slot_index // adp_dev
    local_index = slot_index % adp_dev
    dest_onehot = (owner_group[..., None] == jnp.arange(groups, dtype=jnp.int32)).astype(jnp.int32)
    earlier = jnp.cumsum(dest_onehot, axis=1) - dest_onehot
    row_position = jnp.sum(earlier * dest_onehot, axis=-1)
    target = owner_group * capacity + row_position
    slot_grid = (
        jnp.arange(groups, dtype=jnp.int32)[:, None] * capacity
        + jnp.arange(capacity, dtype=jnp.int32)[None, :]
    )
    placement = (target[:, None, None, :] == slot_grid[None, :, :, None]).astype(jnp.bfloat16)
    send_rows = jnp.einsum(
        "sgcr,srf->gscf", placement, step_acts, preferred_element_type=jnp.float32
    ).astype(jnp.bfloat16)
    local_onehot = (local_index[..., None] == jnp.arange(adp_dev, dtype=jnp.int32)).astype(
        jnp.bfloat16
    )
    send_select = jnp.einsum(
        "sgcr,sra->gsca", placement, local_onehot, preferred_element_type=jnp.float32
    ).astype(jnp.bfloat16)
    rows_in = lax.all_to_all(send_rows, "ad", split_axis=0, concat_axis=0, tiled=True)
    select_in = lax.all_to_all(send_select, "ad", split_axis=0, concat_axis=0, tiled=True)
    owner_delta = owner_blocks(rows_in, select_in, shrink_weight, expand_weight)
    returned = lax.all_to_all(owner_delta, "ad", split_axis=0, concat_axis=0, tiled=True)
    delta_back = jnp.einsum(
        "sgcr,gscf->srf", placement, returned, preferred_element_type=jnp.float32
    )
    base_rows = base_out.reshape(step_count, row_count, base_weight.shape[1])
    return (base_rows + delta_back).astype(jnp.bfloat16)


def body(activations, adapter_ids, owner_slots, base_weight, shrink_weight, expand_weight):

    def one_step(carry_value, inputs):
        step_acts, step_ids = inputs
        step_out = apply_steps(
            step_acts[None], step_ids[None], owner_slots, base_weight, shrink_weight, expand_weight
        )
        return (carry_value, step_out[0])

    carry_value, result = lax.scan(one_step, jnp.int32(0), (activations, adapter_ids))
    return result


def solution(mesh):
    in_specs = (
        P(None, ("rep", "ad"), "tp"),
        P(None, ("rep", "ad")),
        P("rep"),
        P(None, "tp"),
        P(("rep", "ad"), "tp", None),
        P(("rep", "ad"), None, "tp"),
    )
    out_specs = P(None, ("rep", "ad"), "tp")
    return jax.shard_map(body, mesh=mesh, in_specs=in_specs, out_specs=out_specs, check_vma=False)
```

profile of v0, /device:TPU:0, one launch (start us, length us, event | category | flops | bytes accessed | tf_op | source)
XLA Modules:
  0.0 698.6 jit_solution(13778285150700192908)
XLA Ops:
  6.5 685.5 %while.13 = (s32[]{:T(128)}, bf16[4,128,2048]{2,1,0:T(8,128)(2,1)}, bf16[4,128,2048]{2,1,0:T(8,128)(2,1)}, bf16[8192,2048]{1,0:T(8,128)(2,1)}, s32[4,128]{1,0:T(...) while((s32[]{:T(128)}, bf16[4,128,2048]{2,1,0:T(8,128)(2,1)}, ...), condition=%wide.region_14.15_spmd, body=%wide.region_0.14_spmd.sunk | while | flops 4971695616 | bytes 150263792 | solution.py:107
  43.2 31.1 %compare_select_fusion.36 = s32[256]{0:T(256)S(1)} fusion(s32[256]{0:T(256)S(1)} %gather_fusion.1, pred[256]{0:T(512)(128)(4,1)S(1)} %get-tuple-element.420, pred[256]{0:T(512)(128)(4,1)S(1)} %get-tuple-element.421, pred[256]{0:T(512)(128)(4,1)S(1)} %get-tuple-element.422, pred[256]{0:T(512)(128)(4,1)S(1)} %get-tuple-element.423, ...), kind=kLoop, calls=%fused_computation.92.clone.1 | loop fusion | flops 13824 | bytes 10696 | tf_op jit(solution)/shard_map/while/body/eval_jaxpr/jit(_where)/select_n | solution.py:28
  85.5 9.7 %gather_fusion = bf16[48,64,2048]{2,1,0:T(8,128)(2,1)} fusion(bf16[32,64,2048]{2,1,0:T(8,128)(2,1)} %get-tuple-element.535, s32[1024]{0:T(1024)S(1)} %pad_clamp_fusion.6), kind=kCustom, calls=%fused_computation.2.clone.1 | custom fusion | bytes 25166016 | tf_op jit(solution)/shard_map/while/body/eval_jaxpr/gather | solution.py:43
  106.5 14.7 %all-reduce.1 = bf16[48,16,64]{2,1,0:T(8,128)(2,1)} all-reduce(f32[48,16,64]{2,1,0:T(8,128)S(1)} %fusion.101), channel_id=1, replica_groups=mesh['rep'=2,'ad'=4,'tp'=4] {'tp'}, use_global_device_ids=true, to_apply=%region_13.13 | all-reduce | flops 49152 | bytes 294912 | tf_op jit(solution)/shard_map/while/body/eval_jaxpr/psum | solution.py:42
  137.9 26.0 %all-to-all-done.2 = bf16[4,1,64,2048]{3,2,1,0:T(8,128)(2,1)S(1)} async-done(((bf16[4,1,64,2048]{3,2,1,0:T(8,128)(2,1)}), bf16[4,1,64,2048]{3,2,1,0:T(8,128)(2,1)S(1)}, u32[]{:S(2)}, u32[]{:S(2)}) %all-to-all-start.2) | async-done | bytes 1048608 | tf_op jit(solution)/shard_map/while/body/eval_jaxpr/all_to_all | solution.py:90
  164.4 16.5 %fusion.102 = bf16[4,128,2048]{2,1,0:T(8,128)(2,1)} fusion(bf16[4,128,2048]{2,1,0:T(8,128)(2,1)} %get-tuple-element.518, s32[]{:T(128)S(6)} %copy.29, f32[128,2048]{1,0:T(8,128)S(1)} %convolution_bitcast_fusion.2, bf16[8192,2048]{1,0:T(8,128)(2,1)} %get-tuple-element.531, bf16[1,128,8192]{2,1,0:T(8,128)(2,1)} %all-gather.5.cloned.1.call-done), kind=kOutput, calls=%fused_computation.13.clone.1 | convolution fusion | flops 4295491584 | bytes 37224452 | tf_op jit(solution)/shard_map/while/body/eval_jaxpr/dot_general | solution.py:60
  214.4 31.1 %compare_select_fusion.36 = s32[256]{0:T(256)S(1)} fusion(s32[256]{0:T(256)S(1)} %gather_fusion.1, pred[256]{0:T(512)(128)(4,1)S(1)} %get-tuple-element.420, pred[256]{0:T(512)(128)(4,1)S(1)} %get-tuple-element.421, pred[256]{0:T(512)(128)(4,1)S(1)} %get-tuple-element.422, pred[256]{0:T(512)(128)(4,1)S(1)} %get-tuple-element.423, ...), kind=kLoop, calls=%fused_computation.92.clone.1 | loop fusion | flops 13824 | bytes 10696 | tf_op jit(solution)/shard_map/while/body/eval_jaxpr/jit(_where)/select_n | solution.py:28
  247.1 9.6 %gather_fusion.2 = bf16[48,2048,64]{1,2,0:T(8,128)(2,1)} fusion(bf16[32,2048,64]{1,2,0:T(8,128)(2,1)} %get-tuple-element.534, s32[1024]{0:T(1024)S(1)} %pad_clamp_fusion.6), kind=kCustom, calls=%fused_computation.1.clone.1 | custom fusion | bytes 25166016 | tf_op jit(solution)/shard_map/while/body/eval_jaxpr/gather | solution.py:38
  256.7 9.7 %gather_fusion = bf16[48,64,2048]{2,1,0:T(8,128)(2,1)} fusion(bf16[32,64,2048]{2,1,0:T(8,128)(2,1)} %get-tuple-element.535, s32[1024]{0:T(1024)S(1)} %pad_clamp_fusion.6), kind=kCustom, calls=%fused_computation.2.clone.1 | custom fusion | bytes 25166016 | tf_op jit(solution)/shard_map/while/body/eval_jaxpr/gather | solution.py:43
  277.7 15.0 %all-reduce.1 = bf16[48,16,64]{2,1,0:T(8,128)(2,1)} all-reduce(f32[48,16,64]{2,1,0:T(8,128)S(1)} %fusion.101), channel_id=1, replica_groups=mesh['rep'=2,'ad'=4,'tp'=4] {'tp'}, use_global_device_ids=true, to_apply=%region_13.13 | all-reduce | flops 49152 | bytes 294912 | tf_op jit(solution)/shard_map/while/body/eval_jaxpr/psum | solution.py:42
  309.0 24.3 %all-to-all-done.2 = bf16[4,1,64,2048]{3,2,1,0:T(8,128)(2,1)S(1)} async-done(((bf16[4,1,64,2048]{3,2,1,0:T(8,128)(2,1)}), bf16[4,1,64,2048]{3,2,1,0:T(8,128)(2,1)S(1)}, u32[]{:S(2)}, u32[]{:S(2)}) %all-to-all-start.2) | async-done | bytes 1048608 | tf_op jit(solution)/shard_map/while/body/eval_jaxpr/all_to_all | solution.py:90
  333.8 16.5 %fusion.102 = bf16[4,128,2048]{2,1,0:T(8,128)(2,1)} fusion(bf16[4,128,2048]{2,1,0:T(8,128)(2,1)} %get-tuple-element.518, s32[]{:T(128)S(6)} %copy.29, f32[128,2048]{1,0:T(8,128)S(1)} %convolution_bitcast_fusion.2, bf16[8192,2048]{1,0:T(8,128)(2,1)} %get-tuple-element.531, bf16[1,128,8192]{2,1,0:T(8,128)(2,1)} %all-gather.5.cloned.1.call-done), kind=kOutput, calls=%fused_computation.13.clone.1 | convolution fusion | flops 4295491584 | bytes 37224452 | tf_op jit(solution)/shard_map/while/body/eval_jaxpr/dot_general | solution.py:60
  383.9 31.1 %compare_select_fusion.36 = s32[256]{0:T(256)S(1)} fusion(s32[256]{0:T(256)S(1)} %gather_fusion.1, pred[256]{0:T(512)(128)(4,1)S(1)} %get-tuple-element.420, pred[256]{0:T(512)(128)(4,1)S(1)} %get-tuple-element.421, pred[256]{0:T(512)(128)(4,1)S(1)} %get-tuple-element.422, pred[256]{0:T(512)(128)(4,1)S(1)} %get-tuple-element.423, ...), kind=kLoop, calls=%fused_computation.92.clone.1 | loop fusion | flops 13824 | bytes 10696 | tf_op jit(solution)/shard_map/while/body/eval_jaxpr/jit(_where)/select_n | solution.py:28
  416.5 9.6 %gather_fusion.2 = bf16[48,2048,64]{1,2,0:T(8,128)(2,1)} fusion(bf16[32,2048,64]{1,2,0:T(8,128)(2,1)} %get-tuple-element.534, s32[1024]{0:T(1024)S(1)} %pad_clamp_fusion.6), kind=kCustom, calls=%fused_computation.1.clone.1 | custom fusion | bytes 25166016 | tf_op jit(solution)/shard_map/while/body/eval_jaxpr/gather | solution.py:38
  426.1 9.7 %gather_fusion = bf16[48,64,2048]{2,1,0:T(8,128)(2,1)} fusion(bf16[32,64,2048]{2,1,0:T(8,128)(2,1)} %get-tuple-element.535, s32[1024]{0:T(1024)S(1)} %pad_clamp_fusion.6), kind=kCustom, calls=%fused_computation.2.clone.1 | custom fusion | bytes 25166016 | tf_op jit(solution)/shard_map/while/body/eval_jaxpr/gather | solution.py:43
  447.2 16.2 %all-reduce.1 = bf16[48,16,64]{2,1,0:T(8,128)(2,1)} all-reduce(f32[48,16,64]{2,1,0:T(8,128)S(1)} %fusion.101), channel_id=1, replica_groups=mesh['rep'=2,'ad'=4,'tp'=4] {'tp'}, use_global_device_ids=true, to_apply=%region_13.13 | all-reduce | flops 49152 | bytes 294912 | tf_op jit(solution)/shard_map/while/body/eval_jaxpr/psum | solution.py:42
  479.7 26.0 %all-to-all-done.2 = bf16[4,1,64,2048]{3,2,1,0:T(8,128)(2,1)S(1)} async-done(((bf16[4,1,64,2048]{3,2,1,0:T(8,128)(2,1)}), bf16[4,1,64,2048]{3,2,1,0:T(8,128)(2,1)S(1)}, u32[]{:S(2)}, u32[]{:S(2)}) %all-to-all-start.2) | async-done | bytes 1048608 | tf_op jit(solution)/shard_map/while/body/eval_jaxpr/all_to_all | solution.py:90
  506.2 16.5 %fusion.102 = bf16[4,128,2048]{2,1,0:T(8,128)(2,1)} fusion(bf16[4,128,2048]{2,1,0:T(8,128)(2,1)} %get-tuple-element.518, s32[]{:T(128)S(6)} %copy.29, f32[128,2048]{1,0:T(8,128)S(1)} %convolution_bitcast_fusion.2, bf16[8192,2048]{1,0:T(8,128)(2,1)} %get-tuple-element.531, bf16[1,128,8192]{2,1,0:T(8,128)(2,1)} %all-gather.5.cloned.1.call-done), kind=kOutput, calls=%fused_computation.13.clone.1 | convolution fusion | flops 4295491584 | bytes 37224452 | tf_op jit(solution)/shard_map/while/body/eval_jaxpr/dot_general | solution.py:60
  556.2 31.1 %compare_select_fusion.36 = s32[256]{0:T(256)S(1)} fusion(s32[256]{0:T(256)S(1)} %gather_fusion.1, pred[256]{0:T(512)(128)(4,1)S(1)} %get-tuple-element.420, pred[256]{0:T(512)(128)(4,1)S(1)} %get-tuple-element.421, pred[256]{0:T(512)(128)(4,1)S(1)} %get-tuple-element.422, pred[256]{0:T(512)(128)(4,1)S(1)} %get-tuple-element.423, ...), kind=kLoop, calls=%fused_computation.92.clone.1 | loop fusion | flops 13824 | bytes 10696 | tf_op jit(solution)/shard_map/while/body/eval_jaxpr/jit(_where)/select_n | solution.py:28
  588.8 9.6 %gather_fusion.2 = bf16[48,2048,64]{1,2,0:T(8,128)(2,1)} fusion(bf16[32,2048,64]{1,2,0:T(8,128)(2,1)} %get-tuple-element.534, s32[1024]{0:T(1024)S(1)} %pad_clamp_fusion.6), kind=kCustom, calls=%fused_computation.1.clone.1 | custom fusion | bytes 25166016 | tf_op jit(solution)/shard_map/while/body/eval_jaxpr/gather | solution.py:38
  598.5 9.7 %gather_fusion = bf16[48,64,2048]{2,1,0:T(8,128)(2,1)} fusion(bf16[32,64,2048]{2,1,0:T(8,128)(2,1)} %get-tuple-element.535, s32[1024]{0:T(1024)S(1)} %pad_clamp_fusion.6), kind=kCustom, calls=%fused_computation.2.clone.1 | custom fusion | bytes 25166016 | tf_op jit(solution)/shard_map/while/body/eval_jaxpr/gather | solution.py:43
  619.5 15.0 %all-reduce.1 = bf16[48,16,64]{2,1,0:T(8,128)(2,1)} all-reduce(f32[48,16,64]{2,1,0:T(8,128)S(1)} %fusion.101), channel_id=1, replica_groups=mesh['rep'=2,'ad'=4,'tp'=4] {'tp'}, use_global_device_ids=true, to_apply=%region_13.13 | all-reduce | flops 49152 | bytes 294912 | tf_op jit(solution)/shard_map/while/body/eval_jaxpr/psum | solution.py:42
  650.8 24.3 %all-to-all-done.2 = bf16[4,1,64,2048]{3,2,1,0:T(8,128)(2,1)S(1)} async-done(((bf16[4,1,64,2048]{3,2,1,0:T(8,128)(2,1)}), bf16[4,1,64,2048]{3,2,1,0:T(8,128)(2,1)S(1)}, u32[]{:S(2)}, u32[]{:S(2)}) %all-to-all-start.2) | async-done | bytes 1048608 | tf_op jit(solution)/shard_map/while/body/eval_jaxpr/all_to_all | solution.py:90
  675.6 16.5 %fusion.102 = bf16[4,128,2048]{2,1,0:T(8,128)(2,1)} fusion(bf16[4,128,2048]{2,1,0:T(8,128)(2,1)} %get-tuple-element.518, s32[]{:T(128)S(6)} %copy.29, f32[128,2048]{1,0:T(8,128)S(1)} %convolution_bitcast_fusion.2, bf16[8192,2048]{1,0:T(8,128)(2,1)} %get-tuple-element.531, bf16[1,128,8192]{2,1,0:T(8,128)(2,1)} %all-gather.5.cloned.1.call-done), kind=kOutput, calls=%fused_computation.13.clone.1 | convolution fusion | flops 4295491584 | bytes 37224452 | tf_op jit(solution)/shard_map/while/body/eval_jaxpr/dot_general | solution.py:60
  (250 shorter events, 264.9 us)
Async XLA Ops:
  9.6 11.9 %all-to-all-start = ((bf16[4,2,1024]{2,1,0:T(2,128)(2,1)}), bf16[4,2,1024]{2,1,0:T(2,128)(2,1)S(1)}, u32[]{:S(2)}, u32[]{:S(2)}) async-start(bf16[4,2,1024]{2,1,0:T(2,128)(2,1)} %reshape.823), calls=%async_computation | async-start | bytes 32768 | tf_op jit(solution)/shard_map/while/body/eval_jaxpr/all_to_all | solution.py:88
  15.9 148.5 %all-gather.5.cloned.1.call-start = ((), (), s32[]{:S(2)}) async-start(), calls=%async_computation.3 | async-start | bytes 2621440 | tf_op jit(solution)/shard_map/while/body/eval_jaxpr/all_gather | solution.py:61
  21.5 73.7 %all-to-all-start.1 = ((bf16[4,1,64,2048]{3,2,1,0:T(8,128)(2,1)}), bf16[4,1,64,2048]{3,2,1,0:T(8,128)(2,1)S(1)}, u32[]{:S(2)}, u32[]{:S(2)}) async-start(bf16[4,1,64,2048]{3,2,1,0:T(8,128)(2,1)} %fusion.100), calls=%async_computation.1 | async-start | bytes 2097152 | tf_op jit(solution)/shard_map/while/body/eval_jaxpr/all_to_all | solution.py:87
  95.2 1.0 copy-start
  132.4 31.5 %all-to-all-start.2 = ((bf16[4,1,64,2048]{3,2,1,0:T(8,128)(2,1)}), bf16[4,1,64,2048]{3,2,1,0:T(8,128)(2,1)S(1)}, u32[]{:S(2)}, u32[]{:S(2)}) async-start(bf16[4,1,64,2048]{3,2,1,0:T(8,128)(2,1)} %broadcast_select_fusion.5), calls=%async_computation.2 | async-start | bytes 2097152 | tf_op jit(solution)/shard_map/while/body/eval_jaxpr/all_to_all | solution.py:90
  183.9 8.8 %all-to-all-start = ((bf16[4,2,1024]{2,1,0:T(2,128)(2,1)}), bf16[4,2,1024]{2,1,0:T(2,128)(2,1)S(1)}, u32[]{:S(2)}, u32[]{:S(2)}) async-start(bf16[4,2,1024]{2,1,0:T(2,128)(2,1)} %reshape.823), calls=%async_computation | async-start | bytes 32768 | tf_op jit(solution)/shard_map/while/body/eval_jaxpr/all_to_all | solution.py:88
  187.2 146.6 %all-gather.5.cloned.1.call-start = ((), (), s32[]{:S(2)}) async-start(), calls=%async_computation.3 | async-start | bytes 2621440 | tf_op jit(solution)/shard_map/while/body/eval_jaxpr/all_gather | solution.py:61
  192.7 73.7 %all-to-all-start.1 = ((bf16[4,1,64,2048]{3,2,1,0:T(8,128)(2,1)}), bf16[4,1,64,2048]{3,2,1,0:T(8,128)(2,1)S(1)}, u32[]{:S(2)}, u32[]{:S(2)}) async-start(bf16[4,1,64,2048]{3,2,1,0:T(8,128)(2,1)} %fusion.100), calls=%async_computation.1 | async-start | bytes 2097152 | tf_op jit(solution)/shard_map/while/body/eval_jaxpr/all_to_all | solution.py:87
  266.5 1.0 copy-start
  303.9 29.4 %all-to-all-start.2 = ((bf16[4,1,64,2048]{3,2,1,0:T(8,128)(2,1)}), bf16[4,1,64,2048]{3,2,1,0:T(8,128)(2,1)S(1)}, u32[]{:S(2)}, u32[]{:S(2)}) async-start(bf16[4,1,64,2048]{3,2,1,0:T(8,128)(2,1)} %broadcast_select_fusion.5), calls=%async_computation.2 | async-start | bytes 2097152 | tf_op jit(solution)/shard_map/while/body/eval_jaxpr/all_to_all | solution.py:90
  353.3 8.8 %all-to-all-start = ((bf16[4,2,1024]{2,1,0:T(2,128)(2,1)}), bf16[4,2,1024]{2,1,0:T(2,128)(2,1)S(1)}, u32[]{:S(2)}, u32[]{:S(2)}) async-start(bf16[4,2,1024]{2,1,0:T(2,128)(2,1)} %reshape.823), calls=%async_computation | async-start | bytes 32768 | tf_op jit(solution)/shard_map/while/body/eval_jaxpr/all_to_all | solution.py:88
  356.6 149.6 %all-gather.5.cloned.1.call-start = ((), (), s32[]{:S(2)}) async-start(), calls=%async_computation.3 | async-start | bytes 2621440 | tf_op jit(solution)/shard_map/while/body/eval_jaxpr/all_gather | solution.py:61
  362.2 73.7 %all-to-all-start.1 = ((bf16[4,1,64,2048]{3,2,1,0:T(8,128)(2,1)}), bf16[4,1,64,2048]{3,2,1,0:T(8,128)(2,1)S(1)}, u32[]{:S(2)}, u32[]{:S(2)}) async-start(bf16[4,1,64,2048]{3,2,1,0:T(8,128)(2,1)} %fusion.100), calls=%async_computation.1 | async-start | bytes 2097152 | tf_op jit(solution)/shard_map/while/body/eval_jaxpr/all_to_all | solution.py:87
  435.9 1.0 copy-start
  474.6 31.1 %all-to-all-start.2 = ((bf16[4,1,64,2048]{3,2,1,0:T(8,128)(2,1)}), bf16[4,1,64,2048]{3,2,1,0:T(8,128)(2,1)S(1)}, u32[]{:S(2)}, u32[]{:S(2)}) async-start(bf16[4,1,64,2048]{3,2,1,0:T(8,128)(2,1)} %broadcast_select_fusion.5), calls=%async_computation.2 | async-start | bytes 2097152 | tf_op jit(solution)/shard_map/while/body/eval_jaxpr/all_to_all | solution.py:90
  525.7 8.8 %all-to-all-start = ((bf16[4,2,1024]{2,1,0:T(2,128)(2,1)}), bf16[4,2,1024]{2,1,0:T(2,128)(2,1)S(1)}, u32[]{:S(2)}, u32[]{:S(2)}) async-start(bf16[4,2,1024]{2,1,0:T(2,128)(2,1)} %reshape.823), calls=%async_computation | async-start | bytes 32768 | tf_op jit(solution)/shard_map/while/body/eval_jaxpr/all_to_all | solution.py:88
  528.9 146.6 %all-gather.5.cloned.1.call-start = ((), (), s32[]{:S(2)}) async-start(), calls=%async_computation.3 | async-start | bytes 2621440 | tf_op jit(solution)/shard_map/while/body/eval_jaxpr/all_gather | solution.py:61
  534.5 73.7 %all-to-all-start.1 = ((bf16[4,1,64,2048]{3,2,1,0:T(8,128)(2,1)}), bf16[4,1,64,2048]{3,2,1,0:T(8,128)(2,1)S(1)}, u32[]{:S(2)}, u32[]{:S(2)}) async-start(bf16[4,1,64,2048]{3,2,1,0:T(8,128)(2,1)} %fusion.100), calls=%async_computation.1 | async-start | bytes 2097152 | tf_op jit(solution)/shard_map/while/body/eval_jaxpr/all_to_all | solution.py:87
  608.2 1.0 copy-start
  645.7 29.4 %all-to-all-start.2 = ((bf16[4,1,64,2048]{3,2,1,0:T(8,128)(2,1)}), bf16[4,1,64,2048]{3,2,1,0:T(8,128)(2,1)S(1)}, u32[]{:S(2)}, u32[]{:S(2)}) async-start(bf16[4,1,64,2048]{3,2,1,0:T(8,128)(2,1)} %broadcast_select_fusion.5), calls=%async_computation.2 | async-start | bytes 2097152 | tf_op jit(solution)/shard_map/while/body/eval_jaxpr/all_to_all | solution.py:90
Sparse Core Ops, SparseCore 0:
  18.3 24.1 all-gather.4
  189.6 23.0 all-gather.4
  359.0 24.9 all-gather.4
  531.0 23.1 all-gather.4
where the time goes:
time: 703 us; the launch traced here: 699 us
  other arithmetic  190 us (27%)
  local copies, waits for them, and re-layouts  146 us (21%)
  matrix products  130 us (18%)
  waiting for transfers between devices  105 us (15%)
  blocking collectives  60.9 us (9%)
  starting transfers between devices  52.5 us (7%)
  between operations  13.1 us (2%)
    select_n x4, other arithmetic, owner_blocks(): jnp.where(sorted_key < adp_dev, block_start[safe_key] + rank_sorted, limit)  124 us
    all_to_all x4, waiting for transfers between devices, apply_steps(): lax.all_to_all(owner_delta, 'ad', split_axis=0, concat_axis=0, tiled=True)  101 us
    dot_general x4, matrix products, apply_steps(): jnp.dot(lax.all_gather(flat_rows, 'tp', axis=1, tiled=True), base_weight,...  66 us
    psum x4, blocking collectives, owner_blocks(): low_rank = lax.psum(partial_value, 'tp').astype(jnp.bfloat16)  60.9 us
    gather x4, local copies, waits for them, and re-layouts, owner_blocks(): expand_blocks = expand_weight[block_adapter]  39 us
    gather x4, local copies, waits for them, and re-layouts, owner_blocks(): shrink_blocks = shrink_weight[block_adapter]  38.6 us
    dot_general x4, matrix products, owner_blocks(): jnp.einsum('bje,bef->bjf', low_rank, expand_blocks, preferred_element_typ...  25.8 us
    dot_general x4, matrix products, owner_blocks(): jnp.einsum('bjf,bfe->bje', block_rows, shrink_blocks, preferred_element_t...  25.4 us
  transfers between devices with their start and end apart: 16, of which 8 were waited for; matrix products, arithmetic and copies ran while one was open for 55% of the time, Pallas kernels for 0%

commit v1 on v0

v1 whole, which is shorter than its diff:
```python
import jax
import jax.numpy as jnp
from jax import lax
from jax.sharding import PartitionSpec as P


def row_places(slots, adp_dev):
    row_count = slots.shape[-1]
    owner = slots // adp_dev
    index = jnp.arange(row_count, dtype=jnp.int32)
    before = index[None, :] < index[:, None]
    same = owner[..., :, None] == owner[..., None, :]
    place = jnp.sum((same & before).astype(jnp.int32), axis=-1)
    return owner, place


def sum_over_tp(value):
    size = lax.axis_size("tp")
    stride = 1
    while stride < size:
        pairs = [(i, i ^ stride) for i in range(size)]
        value = value + lax.ppermute(value, "tp", pairs)
        stride *= 2
    return value


def body(activations, adapter_ids, owner_slots, base_weight, shrink_weight, expand_weight):
    steps, row_count, width = activations.shape
    adp_dev, _, rank = shrink_weight.shape
    columns = base_weight.shape[1]
    groups = lax.axis_size("ad")
    me = lax.axis_index("ad")
    capacity = row_count // 2

    matches = adapter_ids[..., None] == jnp.arange(owner_slots.shape[0], dtype=jnp.int32)
    slots = jnp.sum(jnp.where(matches, owner_slots, 0), axis=-1)
    owner, place = row_places(slots, adp_dev)
    target = owner * capacity + place
    places = (
        target[:, None, :] == jnp.arange(groups * capacity, dtype=jnp.int32)[None, :, None]
    ).astype(jnp.bfloat16)

    every_slot = lax.all_gather(slots, "ad")
    every_owner, every_place = row_places(every_slot, adp_dev)
    here = jnp.where(every_owner == me, every_place, -1)
    hit = here[:, :, None, :] == jnp.arange(capacity, dtype=jnp.int32)[:, None]
    local = jnp.sum(jnp.where(hit, (every_slot % adp_dev + 1)[:, :, None, :], 0), axis=-1) - 1

    received = []
    for s in range(steps):
        send = jnp.dot(
            places[s], activations[s], preferred_element_type=jnp.float32
        ).astype(jnp.bfloat16)
        send = send.reshape(groups, capacity, width)
        received.append(lax.all_to_all(send, "ad", split_axis=0, concat_axis=0, tiled=True))

    gathered = lax.all_gather(
        activations.reshape(steps * row_count, width), "tp", axis=1, tiled=True
    )
    base_out = jnp.dot(gathered, base_weight, preferred_element_type=jnp.float32)
    base_out = base_out.reshape(steps, row_count, columns)

    down = shrink_weight.transpose(1, 0, 2).reshape(width, adp_dev * rank)
    up = expand_weight.reshape(adp_dev * rank, columns)
    outs = []
    for s in range(steps):
        rows = received[s].reshape(groups * capacity, width)
        mark = local[:, s].reshape(groups * capacity, 1) == jnp.arange(adp_dev, dtype=jnp.int32)
        every = jnp.dot(rows, down, preferred_element_type=jnp.float32)
        every = every.reshape(groups * capacity, adp_dev, rank)
        partial = jnp.sum(jnp.where(mark[..., None], every, 0.0), axis=1)
        low_rank = sum_over_tp(partial).astype(jnp.bfloat16)
        spread = jnp.where(mark[..., None], low_rank[:, None, :], jnp.zeros((), jnp.bfloat16))
        delta = jnp.dot(
            spread.reshape(groups * capacity, adp_dev * rank),
            up,
            preferred_element_type=jnp.float32,
        ).astype(jnp.bfloat16)
        returned = lax.all_to_all(
            delta.reshape(groups, capacity, columns), "ad", split_axis=0, concat_axis=0, tiled=True
        )
        back = jnp.einsum(
            "cr,cf->rf",
            places[s],
            returned.reshape(groups * capacity, columns),
            preferred_element_type=jnp.float32,
        )
        outs.append((base_out[s] + back).astype(jnp.bfloat16))
    return jnp.stack(outs)


def solution(mesh):
    in_specs = (
        P(None, ("rep", "ad"), "tp"),
        P(None, ("rep", "ad")),
        P("rep"),
        P(None, "tp"),
        P(("rep", "ad"), "tp", None),
        P(("rep", "ad"), None, "tp"),
    )
    out_specs = P(None, ("rep", "ad"), "tp")
    return jax.shard_map(body, mesh=mesh, in_specs=in_specs, out_specs=out_specs, check_vma=False)
```

time: 703 us -> 264 us (0.38)
  other arithmetic: 190 us -> 4.19 us
  local copies, waits for them, and re-layouts: 146 us -> 1.76 us
  matrix products: 130 us -> 85.5 us
  blocking collectives: 60.9 us -> 30.5 us
  waiting for transfers between devices: 105 us -> 88.4 us
  starting transfers between devices: 52.5 us -> 39 us
    select_n x28 -> x3, other arithmetic: 134 us -> 0.04 us  [the longest x2 0.03 us: row_places(): owner = slots // adp_dev]
    gather x32 -> x0, local copies, waits for them, and re-layouts: 106 us -> none  [the longest x4 39 us: owner_blocks(): expand_blocks = expand_weight[block_adapter]]
    psum x4 -> x0, blocking collectives: 60.9 us -> none  [owner_blocks(): low_rank = lax.psum(partial_value, 'tp').astype(jnp.bfloat16)]
    dot_general x24 -> x17, matrix products: 130 us -> 85.5 us  [the longest x4 26.9 us: body(): jnp.dot(spread.reshape(groups * capacity, adp_dev * rank), up, preferred_...]
    gather x24 -> x0, other arithmetic: 35.6 us -> none  [the longest x8 18 us: owner_blocks(): block_start[safe_key] + rank_sorted]
    all_gather x0 -> x1, blocking collectives: none -> 30.5 us  [body(): every_slot = lax.all_gather(slots, 'ad')]
    all_to_all x12 -> x8, waiting for transfers between devices: 105 us -> 79.1 us  [the longest x4 46 us: body(): lax.all_to_all(send, 'ad', split_axis=0, concat_axis=0, tiled=True)]
    scatter x8 -> x0, local copies, waits for them, and re-layouts: 21.3 us -> none  [the longest x4 15.7 us: owner_blocks(): jnp.zeros((limit, width_local), rows_in.dtype).at[position]]
  transfers between devices with their start and end apart: 16 -> 17, of which waited for: 8 -> 10; matrix products, arithmetic and copies ran while one was open for 55% -> 31% of each run, Pallas kernels for 0% -> 0%
where the time goes in v1:
time: 264 us; the launch traced here: 263 us
  waiting for transfers between devices  88.4 us (33%)
  matrix products  85.5 us (32%)
  starting transfers between devices  39 us (15%)
  blocking collectives  30.5 us (12%)
  between operations  13.7 us (5%)
  other arithmetic  4.19 us (2%)
    all_to_all x4, waiting for transfers between devices, body(): lax.all_to_all(send, 'ad', split_axis=0, concat_axis=0, tiled=True)  46 us
    all_to_all x4, waiting for transfers between devices, body(): lax.all_to_all(delta.reshape(groups, capacity, columns), 'ad', split_axis...  33.1 us
    all_gather x1, blocking collectives, body(): every_slot = lax.all_gather(slots, 'ad')  30.5 us
    dot_general x4, matrix products, body(): jnp.dot(spread.reshape(groups * capacity, adp_dev * rank), up, preferred_...  26.9 us
    dot_general x4, matrix products, body(): every = jnp.dot(rows, down, preferred_element_type=jnp.float32)  24.2 us
    dot_general x1, matrix products, body(): jnp.dot(gathered, base_weight, preferred_element_type=jnp.float32)  23.8 us
    all_to_all x4, starting transfers between devices, body(): lax.all_to_all(send, 'ad', split_axis=0, concat_axis=0, tiled=True)  17.6 us
    all_to_all x4, starting transfers between devices, body(): lax.all_to_all(delta.reshape(groups, capacity, columns), 'ad', split_axis...  15.2 us
  transfers between devices with their start and end apart: 17, of which 10 were waited for; matrix products, arithmetic and copies ran while one was open for 31% of the time, Pallas kernels for 0%

profile of v1, /device:TPU:0, one launch (start us, length us, event | category | flops | bytes accessed | tf_op | source)
XLA Modules:
  0.0 263.1 jit_solution(15237167639445704751)
XLA Ops:
  10.5 6.3 %all-to-all-start.6 = ((bf16[4,64,2048]{2,1,0:T(8,128)(2,1)}), bf16[4,64,2048]{2,1,0:T(8,128)(2,1)S(1)}, u32[]{:S(2)}, u32[]{:S(2)}) async-start(bf16[4,64,2048]{2,1,0:T(8,128)(2,1)} %bitcast.38), calls=%async_computation.6 | async-start | bytes 2097152 | tf_op jit(solution)/shard_map/all_to_all | solution.py:55
  18.9 23.6 %all-to-all-done.6 = bf16[4,64,2048]{2,1,0:T(8,128)(2,1)S(1)} async-done(((bf16[4,64,2048]{2,1,0:T(8,128)(2,1)}), bf16[4,64,2048]{2,1,0:T(8,128)(2,1)S(1)}, u32[]{:S(2)}, u32[]{:S(2)}) %all-to-all-start.6) | async-done | bytes 1048608 | tf_op jit(solution)/shard_map/all_to_all | solution.py:55
  42.5 4.3 %all-to-all-start.4 = ((bf16[4,64,2048]{2,1,0:T(8,128)(2,1)}), bf16[4,64,2048]{2,1,0:T(8,128)(2,1)}, u32[]{:S(2)}, u32[]{:S(2)}) async-start(bf16[4,64,2048]{2,1,0:T(8,128)(2,1)} %bitcast.29), calls=%async_computation.4 | async-start | bytes 2097152 | tf_op jit(solution)/shard_map/all_to_all | solution.py:55
  46.8 30.5 %all-gather.1 = s32[4,4,128]{2,1,0:T(4,128)S(1)} all-gather(s32[1,4,128]{2,1,0:T(4,128)S(1)} %bitcast.124), channel_id=2, replica_groups=mesh['rep'=2,'ad'=4,'tp'=4] {'ad'}, dimensions={0}, use_global_device_ids=true | all-gather | bytes 10240 | tf_op jit(solution)/shard_map/all_gather | solution.py:43
  79.7 3.5 %all-to-all-start.2 = ((bf16[4,64,2048]{2,1,0:T(8,128)(2,1)}), bf16[4,64,2048]{2,1,0:T(8,128)(2,1)S(1)}, u32[]{:S(2)}, u32[]{:S(2)}) async-start(bf16[4,64,2048]{2,1,0:T(8,128)(2,1)} %bitcast.17), calls=%async_computation.2 | async-start | bytes 2097152 | tf_op jit(solution)/shard_map/all_to_all | solution.py:55
  85.0 6.1 %select_reduce_fusion = f32[256,64]{0,1:T(8,128)S(1)} fusion(bf16[256,2048,1]{1,0,2:T(8,128)(2,1)} %bitcast.121, bf16[32,2048,64]{1,2,0:T(8,128)(2,1)} %param.10, pred[256,32]{0,1:T(8,128)(4,1)S(1)} %iota_compare_fusion.4), kind=kOutput, calls=%fused_computation.33 | convolution fusion | flops 2148515840 | bytes 9510912 | tf_op jit(solution)/shard_map/dot_general | solution.py:69
  91.2 15.1 %all-to-all-done.2 = bf16[4,64,2048]{2,1,0:T(8,128)(2,1)S(1)} async-done(((bf16[4,64,2048]{2,1,0:T(8,128)(2,1)}), bf16[4,64,2048]{2,1,0:T(8,128)(2,1)S(1)}, u32[]{:S(2)}, u32[]{:S(2)}) %all-to-all-start.2) | async-done | bytes 1048608 | tf_op jit(solution)/shard_map/all_to_all | solution.py:55
  106.3 3.5 %all-to-all-start = ((bf16[4,64,2048]{2,1,0:T(8,128)(2,1)}), bf16[4,64,2048]{2,1,0:T(8,128)(2,1)S(1)}, u32[]{:S(2)}, u32[]{:S(2)}) async-start(bf16[4,64,2048]{2,1,0:T(8,128)(2,1)} %bitcast.4), calls=%async_computation | async-start | bytes 2097152 | tf_op jit(solution)/shard_map/all_to_all | solution.py:55
  109.8 6.1 %select_reduce_fusion.1 = f32[256,64]{0,1:T(8,128)S(1)} fusion(bf16[256,2048,1]{1,0,2:T(8,128)(2,1)} %bitcast.31, bf16[32,2048,64]{1,2,0:T(8,128)(2,1)} %param.10, pred[256,32]{0,1:T(8,128)(4,1)S(1)} %iota_compare_fusion.5), kind=kOutput, calls=%fused_computation.34 | convolution fusion | flops 2148515840 | bytes 9510912 | tf_op jit(solution)/shard_map/dot_general | solution.py:69
  120.7 6.7 %fusion.11 = bf16[256,2048]{1,0:T(8,128)(2,1)} fusion(bf16[32,64,2048]{2,1,0:T(8,128)(2,1)} %param.11, pred[256,32]{0,1:T(8,128)(4,1)S(1)} %iota_compare_fusion.4, bf16[256,64]{0,1:T(8,128)(2,1)S(1)} %add_convert_fusion), kind=kOutput, calls=%fused_computation.19 | convolution fusion | flops 2148532224 | bytes 9478144 | tf_op jit(solution)/shard_map/dot_general | solution.py:74
  127.5 7.3 %all-to-all-done = bf16[4,64,2048]{2,1,0:T(8,128)(2,1)S(1)} async-done(((bf16[4,64,2048]{2,1,0:T(8,128)(2,1)}), bf16[4,64,2048]{2,1,0:T(8,128)(2,1)S(1)}, u32[]{:S(2)}, u32[]{:S(2)}) %all-to-all-start) | async-done | bytes 1048608 | tf_op jit(solution)/shard_map/all_to_all | solution.py:55
  135.8 3.7 %all-to-all-start.7 = ((bf16[4,64,2048]{2,1,0:T(8,128)(2,1)}), bf16[4,64,2048]{2,1,0:T(8,128)(2,1)S(1)}, u32[]{:S(2)}, u32[]{:S(2)}) async-start(bf16[4,64,2048]{2,1,0:T(8,128)(2,1)} %bitcast.42), calls=%async_computation.7 | async-start | bytes 2097152 | tf_op jit(solution)/shard_map/all_to_all | solution.py:79
  139.5 5.8 %select_reduce_fusion.2 = f32[256,64]{0,1:T(8,128)S(1)} fusion(bf16[256,2048,1]{1,0,2:T(8,128)(2,1)S(1)} %bitcast.120, bf16[32,2048,64]{1,2,0:T(8,128)(2,1)} %param.10, pred[256,32]{0,1:T(8,128)(4,1)S(1)} %iota_compare_fusion.6), kind=kOutput, calls=%fused_computation.35 | convolution fusion | flops 2148515840 | bytes 9510912 | tf_op jit(solution)/shard_map/dot_general | solution.py:69
  145.5 6.7 %fusion.10 = bf16[256,2048]{1,0:T(8,128)(2,1)} fusion(bf16[32,64,2048]{2,1,0:T(8,128)(2,1)} %param.11, pred[256,32]{0,1:T(8,128)(4,1)S(1)} %iota_compare_fusion.5, bf16[256,64]{0,1:T(8,128)(2,1)S(1)} %add_convert_fusion.1), kind=kOutput, calls=%fused_computation.18 | convolution fusion | flops 2148532224 | bytes 9478144 | tf_op jit(solution)/shard_map/dot_general | solution.py:74
  152.2 12.4 %all-to-all-done.7 = bf16[4,64,2048]{2,1,0:T(8,128)(2,1)S(1)} async-done(((bf16[4,64,2048]{2,1,0:T(8,128)(2,1)}), bf16[4,64,2048]{2,1,0:T(8,128)(2,1)S(1)}, u32[]{:S(2)}, u32[]{:S(2)}) %all-to-all-start.7) | async-done | bytes 1048608 | tf_op jit(solution)/shard_map/all_to_all | solution.py:79
  164.5 3.5 %all-to-all-start.5 = ((bf16[4,64,2048]{2,1,0:T(8,128)(2,1)}), bf16[4,64,2048]{2,1,0:T(8,128)(2,1)S(1)}, u32[]{:S(2)}, u32[]{:S(2)}) async-start(bf16[4,64,2048]{2,1,0:T(8,128)(2,1)} %bitcast.33), calls=%async_computation.5 | async-start | bytes 2097152 | tf_op jit(solution)/shard_map/all_to_all | solution.py:79
  172.5 6.7 %fusion.9 = bf16[256,2048]{1,0:T(8,128)(2,1)} fusion(bf16[32,64,2048]{2,1,0:T(8,128)(2,1)} %param.11, pred[256,32]{0,1:T(8,128)(4,1)S(1)} %iota_compare_fusion.6, bf16[256,64]{0,1:T(8,128)(2,1)S(1)} %add_convert_fusion.2), kind=kOutput, calls=%fused_computation.17 | convolution fusion | flops 2148532224 | bytes 9478144 | tf_op jit(solution)/shard_map/dot_general | solution.py:74
  179.2 14.0 %all-to-all-done.5 = bf16[4,64,2048]{2,1,0:T(8,128)(2,1)S(1)} async-done(((bf16[4,64,2048]{2,1,0:T(8,128)(2,1)}), bf16[4,64,2048]{2,1,0:T(8,128)(2,1)S(1)}, u32[]{:S(2)}, u32[]{:S(2)}) %all-to-all-start.5) | async-done | bytes 1048608 | tf_op jit(solution)/shard_map/all_to_all | solution.py:79
  193.3 3.5 %all-to-all-start.3 = ((bf16[4,64,2048]{2,1,0:T(8,128)(2,1)}), bf16[4,64,2048]{2,1,0:T(8,128)(2,1)S(1)}, u32[]{:S(2)}, u32[]{:S(2)}) async-start(bf16[4,64,2048]{2,1,0:T(8,128)(2,1)} %bitcast.122), calls=%async_computation.3 | async-start | bytes 2097152 | tf_op jit(solution)/shard_map/all_to_all | solution.py:79
  196.8 6.1 %select_reduce_fusion.3 = f32[256,64]{0,1:T(8,128)S(1)} fusion(bf16[256,2048,1]{1,0,2:T(8,128)(2,1)} %bitcast.119, bf16[32,2048,64]{1,2,0:T(8,128)(2,1)} %param.10, pred[256,32]{0,1:T(8,128)(4,1)S(1)} %iota_compare_fusion.7), kind=kOutput, calls=%fused_computation.36 | convolution fusion | flops 2148515840 | bytes 9510912 | tf_op jit(solution)/shard_map/dot_general | solution.py:69
  208.6 6.7 %fusion.8 = bf16[256,2048]{1,0:T(8,128)(2,1)} fusion(bf16[32,64,2048]{2,1,0:T(8,128)(2,1)} %param.11, pred[256,32]{0,1:T(8,128)(4,1)S(1)} %iota_compare_fusion.7, bf16[256,64]{0,1:T(8,128)(2,1)S(1)} %add_convert_fusion.3), kind=kOutput, calls=%fused_computation.16 | convolution fusion | flops 2148532224 | bytes 9478144 | tf_op jit(solution)/shard_map/dot_general | solution.py:74
  215.3 6.7 %all-to-all-done.3 = bf16[4,64,2048]{2,1,0:T(8,128)(2,1)S(1)} async-done(((bf16[4,64,2048]{2,1,0:T(8,128)(2,1)}), bf16[4,64,2048]{2,1,0:T(8,128)(2,1)S(1)}, u32[]{:S(2)}, u32[]{:S(2)}) %all-to-all-start.3) | async-done | bytes 1048608 | tf_op jit(solution)/shard_map/all_to_all | solution.py:79
  222.0 4.5 %all-to-all-start.1 = ((bf16[4,64,2048]{2,1,0:T(8,128)(2,1)}), bf16[4,64,2048]{2,1,0:T(8,128)(2,1)}, u32[]{:S(2)}, u32[]{:S(2)}) async-start(bf16[4,64,2048]{2,1,0:T(8,128)(2,1)} %bitcast.123), calls=%async_computation.1 | async-start | bytes 2097152 | tf_op jit(solution)/shard_map/all_to_all | solution.py:79
  226.5 23.8 %fusion.60 = f32[512,2048]{1,0:T(8,128)S(1)} fusion(bf16[512,8192]{1,0:T(8,128)(2,1)} %all-gather.4.cloned.1.call-done, bf16[8192,2048]{1,0:T(8,128)(2,1)} %param.9), kind=kOutput, calls=%fused_computation.108 | convolution fusion | flops 17179869184 | bytes 46137344 | tf_op jit(solution)/shard_map/dot_general | solution.py:60
  (68 shorter events, 32.2 us)
Async XLA Ops:
  6.5 11.0 %copy-start = (bf16[4,128,2048]{2,1,0:T(8,128)(2,1)S(1)}, bf16[4,128,2048]{2,1,0:T(8,128)(2,1)}, u32[]{:S(2)}) copy-start(bf16[4,128,2048]{2,1,0:T(8,128)(2,1)} %param.6) | copy-start | bytes 6291460
  10.5 32.0 %all-to-all-start.6 = ((bf16[4,64,2048]{2,1,0:T(8,128)(2,1)}), bf16[4,64,2048]{2,1,0:T(8,128)(2,1)S(1)}, u32[]{:S(2)}, u32[]{:S(2)}) async-start(bf16[4,64,2048]{2,1,0:T(8,128)(2,1)} %bitcast.38), calls=%async_computation.6 | async-start | bytes 2097152 | tf_op jit(solution)/shard_map/all_to_all | solution.py:55
  16.8 209.7 %all-gather.4.cloned.1.call-start = ((), (), s32[]{:S(2)}) async-start(), calls=%async_computation.8 | async-start | bytes 10485760 | tf_op jit(solution)/shard_map/all_gather | solution.py:57
  42.5 37.2 %copy-start.4 = (bf16[4,64,2048]{2,1,0:T(8,128)(2,1)}, bf16[4,64,2048]{2,1,0:T(8,128)(2,1)S(1)}, u32[]{:S(2)}) copy-start(bf16[4,64,2048]{2,1,0:T(8,128)(2,1)S(1)} %all-to-all-done.6) | copy-start | bytes 3145732
  42.5 37.2 %all-to-all-start.4 = ((bf16[4,64,2048]{2,1,0:T(8,128)(2,1)}), bf16[4,64,2048]{2,1,0:T(8,128)(2,1)}, u32[]{:S(2)}, u32[]{:S(2)}) async-start(bf16[4,64,2048]{2,1,0:T(8,128)(2,1)} %bitcast.29), calls=%async_computation.4 | async-start | bytes 2097152 | tf_op jit(solution)/shard_map/all_to_all | solution.py:55
  79.7 26.6 %all-to-all-start.2 = ((bf16[4,64,2048]{2,1,0:T(8,128)(2,1)}), bf16[4,64,2048]{2,1,0:T(8,128)(2,1)S(1)}, u32[]{:S(2)}, u32[]{:S(2)}) async-start(bf16[4,64,2048]{2,1,0:T(8,128)(2,1)} %bitcast.17), calls=%async_computation.2 | async-start | bytes 2097152 | tf_op jit(solution)/shard_map/all_to_all | solution.py:55
  91.1 24.9 %collective-permute-start.6 = (f32[256,64]{0,1:T(8,128)S(1)}, f32[256,64]{0,1:T(8,128)S(1)}, u32[]{:S(2)}, u32[]{:S(2)}) collective-permute-start(f32[256,64]{0,1:T(8,128)S(1)} %select_reduce_fusion), channel_id=1, source_target_pairs={{0,1},{1,0},{2,3},{3,2},{4,5},{5,4},{6,7},{7,6},{8,9},{9,8},{10,11... | collective-permute-start | bytes 196616 | tf_op jit(solution)/shard_map/ppermute | solution.py:22
  106.3 28.5 %all-to-all-start = ((bf16[4,64,2048]{2,1,0:T(8,128)(2,1)}), bf16[4,64,2048]{2,1,0:T(8,128)(2,1)S(1)}, u32[]{:S(2)}, u32[]{:S(2)}) async-start(bf16[4,64,2048]{2,1,0:T(8,128)(2,1)} %bitcast.4), calls=%async_computation | async-start | bytes 2097152 | tf_op jit(solution)/shard_map/all_to_all | solution.py:55
  116.0 1.7 collective-permute-start.4
  116.1 4.7 %collective-permute-start.7 = (f32[256,64]{0,1:T(8,128)S(1)}, f32[256,64]{0,1:T(8,128)S(1)}, u32[]{:S(2)}, u32[]{:S(2)}) collective-permute-start(f32[256,64]{0,1:T(8,128)S(1)} %add.79), channel_id=1, source_target_pairs={{0,2},{1,3},{2,0},{3,1},{4,6},{5,7},{6,4},{7,5},{8,10},{9,11},{10,... | collective-permute-start | bytes 196616 | tf_op jit(solution)/shard_map/ppermute | solution.py:22
  117.7 27.7 %collective-permute-start.5 = (f32[256,64]{0,1:T(8,128)S(1)}, f32[256,64]{0,1:T(8,128)S(1)}, u32[]{:S(2)}, u32[]{:S(2)}) collective-permute-start(f32[256,64]{0,1:T(8,128)S(1)} %add.76), channel_id=1, source_target_pairs={{0,2},{1,3},{2,0},{3,1},{4,6},{5,7},{6,4},{7,5},{8,10},{9,11},{10,... | collective-permute-start | bytes 196616 | tf_op jit(solution)/shard_map/ppermute | solution.py:22
  134.8 1.1 copy-start.3
  135.8 28.7 %all-to-all-start.7 = ((bf16[4,64,2048]{2,1,0:T(8,128)(2,1)}), bf16[4,64,2048]{2,1,0:T(8,128)(2,1)S(1)}, u32[]{:S(2)}, u32[]{:S(2)}) async-start(bf16[4,64,2048]{2,1,0:T(8,128)(2,1)} %bitcast.42), calls=%async_computation.7 | async-start | bytes 2097152 | tf_op jit(solution)/shard_map/all_to_all | solution.py:79
  145.3 22.8 %collective-permute-start.2 = (f32[256,64]{0,1:T(8,128)S(1)}, f32[256,64]{0,1:T(8,128)S(1)}, u32[]{:S(2)}, u32[]{:S(2)}) collective-permute-start(f32[256,64]{0,1:T(8,128)S(1)} %select_reduce_fusion.2), channel_id=1, source_target_pairs={{0,1},{1,0},{2,3},{3,2},{4,5},{5,4},{6,7},{7,6},{8,9},{9,8},{10,11... | collective-permute-start | bytes 196616 | tf_op jit(solution)/shard_map/ppermute | solution.py:22
  164.5 28.7 %all-to-all-start.5 = ((bf16[4,64,2048]{2,1,0:T(8,128)(2,1)}), bf16[4,64,2048]{2,1,0:T(8,128)(2,1)S(1)}, u32[]{:S(2)}, u32[]{:S(2)}) async-start(bf16[4,64,2048]{2,1,0:T(8,128)(2,1)} %bitcast.33), calls=%async_computation.5 | async-start | bytes 2097152 | tf_op jit(solution)/shard_map/all_to_all | solution.py:79
  168.2 4.3 %collective-permute-start.3 = (f32[256,64]{0,1:T(8,128)S(1)}, f32[256,64]{0,1:T(8,128)S(1)}, u32[]{:S(2)}, u32[]{:S(2)}) collective-permute-start(f32[256,64]{0,1:T(8,128)S(1)} %add.73), channel_id=1, source_target_pairs={{0,2},{1,3},{2,0},{3,1},{4,6},{5,7},{6,4},{7,5},{8,10},{9,11},{10,... | collective-permute-start | bytes 196616 | tf_op jit(solution)/shard_map/ppermute | solution.py:22
  193.3 28.7 %all-to-all-start.3 = ((bf16[4,64,2048]{2,1,0:T(8,128)(2,1)}), bf16[4,64,2048]{2,1,0:T(8,128)(2,1)S(1)}, u32[]{:S(2)}, u32[]{:S(2)}) async-start(bf16[4,64,2048]{2,1,0:T(8,128)(2,1)} %bitcast.122), calls=%async_computation.3 | async-start | bytes 2097152 | tf_op jit(solution)/shard_map/all_to_all | solution.py:79
  202.9 1.3 collective-permute-start
  204.2 4.3 %collective-permute-start.1 = (f32[256,64]{0,1:T(8,128)S(1)}, f32[256,64]{0,1:T(8,128)S(1)}, u32[]{:S(2)}, u32[]{:S(2)}) collective-permute-start(f32[256,64]{0,1:T(8,128)S(1)} %add.70), channel_id=1, source_target_pairs={{0,2},{1,3},{2,0},{3,1},{4,6},{5,7},{6,4},{7,5},{8,10},{9,11},{10,... | collective-permute-start | bytes 196616 | tf_op jit(solution)/shard_map/ppermute | solution.py:22
  222.0 30.8 %all-to-all-start.1 = ((bf16[4,64,2048]{2,1,0:T(8,128)(2,1)}), bf16[4,64,2048]{2,1,0:T(8,128)(2,1)}, u32[]{:S(2)}, u32[]{:S(2)}) async-start(bf16[4,64,2048]{2,1,0:T(8,128)(2,1)} %bitcast.123), calls=%async_computation.1 | async-start | bytes 2097152 | tf_op jit(solution)/shard_map/all_to_all | solution.py:79
  250.3 2.2 copy-start.1
  251.7 3.0 %copy-start.2 = (bf16[1,128,2048]{2,1,0:T(8,128)(2,1)S(1)}, bf16[1,128,2048]{2,1,0:T(8,128)(2,1)}, u32[]{:S(2)}) copy-start(bf16[1,128,2048]{2,1,0:T(8,128)(2,1)} %fusion.16) | copy-start | bytes 1572868
Sparse Core Ops, SparseCore 0:
  19.2 59.7 all-gather.3

commit v2 on v1

--- a/solution.py
+++ b/solution.py
@@ -35,16 +35,18 @@
     matches = adapter_ids[..., None] == jnp.arange(owner_slots.shape[0], dtype=jnp.int32)
     slots = jnp.sum(jnp.where(matches, owner_slots, 0), axis=-1)
     owner, place = row_places(slots, adp_dev)
-    target = owner * capacity + place
-    places = (
-        target[:, None, :] == jnp.arange(groups * capacity, dtype=jnp.int32)[None, :, None]
-    ).astype(jnp.bfloat16)
+    target = lax.rem(owner - me + groups, groups) * capacity + place
+    hit = target[:, None, :] == jnp.arange(groups * capacity, dtype=jnp.int32)[None, :, None]
+    places = hit.astype(jnp.bfloat16)
+    marks = jnp.sum(jnp.where(hit, (slots % adp_dev + 1)[:, None, :], 0), axis=-1) - 1
+    marks = marks.reshape(steps, groups, capacity)
 
-    every_slot = lax.all_gather(slots, "ad")
-    every_owner, every_place = row_places(every_slot, adp_dev)
-    here = jnp.where(every_owner == me, every_place, -1)
-    hit = here[:, :, None, :] == jnp.arange(capacity, dtype=jnp.int32)[:, None]
-    local = jnp.sum(jnp.where(hit, (every_slot % adp_dev + 1)[:, :, None, :], 0), axis=-1) - 1
+    def shifted(block, k):
+        if k % groups == 0:
+            return block
+        return lax.ppermute(block, "ad", [(i, (i + k) % groups) for i in range(groups)])
+
+    local = jnp.stack([shifted(marks[:, k], k) for k in range(groups)], axis=1)
 
     received = []
     for s in range(steps):
@@ -52,7 +54,7 @@
             places[s], activations[s], preferred_element_type=jnp.float32
         ).astype(jnp.bfloat16)
         send = send.reshape(groups, capacity, width)
-        received.append(lax.all_to_all(send, "ad", split_axis=0, concat_axis=0, tiled=True))
+        received.append(jnp.concatenate([shifted(send[k], k) for k in range(groups)]))
 
     gathered = lax.all_gather(
         activations.reshape(steps * row_count, width), "tp", axis=1, tiled=True
@@ -64,8 +66,8 @@
     up = expand_weight.reshape(adp_dev * rank, columns)
     outs = []
     for s in range(steps):
-        rows = received[s].reshape(groups * capacity, width)
-        mark = local[:, s].reshape(groups * capacity, 1) == jnp.arange(adp_dev, dtype=jnp.int32)
+        rows = received[s]
+        mark = local[s].reshape(groups * capacity, 1) == jnp.arange(adp_dev, dtype=jnp.int32)
         every = jnp.dot(rows, down, preferred_element_type=jnp.float32)
         every = every.reshape(groups * capacity, adp_dev, rank)
         partial = jnp.sum(jnp.where(mark[..., None], every, 0.0), axis=1)
@@ -76,13 +78,12 @@
             up,
             preferred_element_type=jnp.float32,
         ).astype(jnp.bfloat16)
-        returned = lax.all_to_all(
-            delta.reshape(groups, capacity, columns), "ad", split_axis=0, concat_axis=0, tiled=True
-        )
+        delta = delta.reshape(groups, capacity, columns)
+        returned = jnp.concatenate([shifted(delta[k], groups - k) for k in range(groups)])
         back = jnp.einsum(
             "cr,cf->rf",
             places[s],
-            returned.reshape(groups * capacity, columns),
+            returned,
             preferred_element_type=jnp.float32,
         )
         outs.append((base_out[s] + back).astype(jnp.bfloat16))

time: 264 us -> 219 us (0.83)
  starting transfers between devices: 39 us -> 74.8 us
  blocking collectives: 30.5 us -> 0 us
  matrix products: 85.5 us -> 56.6 us
  waiting for transfers between devices: 88.4 us -> 66.3 us
    all_to_all x8 -> x0, waiting for transfers between devices: 79.1 us -> none  [the longest x4 46 us: body(): lax.all_to_all(send, 'ad', split_axis=0, concat_axis=0, tiled=True)]
    ppermute x0 -> x27, starting transfers between devices: none -> 69.8 us  [shifted(): lax.ppermute(block, 'ad', [(i, (i + k) % groups) for i in range(groups)])]
    ppermute x0 -> x27, waiting for transfers between devices: none -> 65.3 us  [shifted(): lax.ppermute(block, 'ad', [(i, (i + k) % groups) for i in range(groups)])]
    all_to_all x8 -> x0, starting transfers between devices: 32.8 us -> none  [the longest x4 17.6 us: body(): lax.all_to_all(send, 'ad', split_axis=0, concat_axis=0, tiled=True)]
    all_gather x1 -> x0, blocking collectives: 30.5 us -> none  [body(): every_slot = lax.all_gather(slots, 'ad')]
    dot_general x4, matrix products: 26.9 us -> 9.53 us  [body(): jnp.dot(spread.reshape(groups * capacity, adp_dev * rank), up, preferred_...]
    ppermute x8, waiting for transfers between devices: 8.6 us -> 0.34 us  [sum_over_tp(): value = value + lax.ppermute(value, 'tp', pairs)]
    dot_general x4, matrix products: 24.2 us -> 17.1 us  [body(): every = jnp.dot(rows, down, preferred_element_type=jnp.float32)]
  transfers between devices with their start and end apart: 17 -> 36, of which waited for: 10 -> 8; matrix products, arithmetic and copies ran while one was open for 31% -> 28% of each run, Pallas kernels for 0% -> 0%
where the time goes in v2:
time: 219 us
  starting transfers between devices  74.8 us (34%)
  waiting for transfers between devices  66.3 us (30%)
  matrix products  56.6 us (26%)
  between operations  13.9 us (6%)
  local copies, waits for them, and re-layouts  4.36 us (2%)
  other arithmetic  2.58 us (1%)
    ppermute x27, starting transfers between devices, shifted(): lax.ppermute(block, 'ad', [(i, (i + k) % groups) for i in range(groups)])  69.8 us
    ppermute x27, waiting for transfers between devices, shifted(): lax.ppermute(block, 'ad', [(i, (i + k) % groups) for i in range(groups)])  65.3 us
    dot_general x1, matrix products, body(): jnp.dot(gathered, base_weight, preferred_element_type=jnp.float32)  23.8 us
    dot_general x4, matrix products, body(): every = jnp.dot(rows, down, preferred_element_type=jnp.float32)  17.1 us
    dot_general x4, matrix products, body(): jnp.dot(spread.reshape(groups * capacity, adp_dev * rank), up, preferred_...  9.53 us
    ppermute x8, starting transfers between devices, sum_over_tp(): value = value + lax.ppermute(value, 'tp', pairs)  4.99 us
    dot_general x4, matrix products, body(): jnp.einsum('cr,cf->rf', places[s], returned, preferred_element_type=jnp.f...  4.42 us
  transfers between devices with their start and end apart: 36, of which 8 were waited for; matrix products, arithmetic and copies ran while one was open for 28% of the time, Pallas kernels for 0%

profile of v2, /device:TPU:0, one launch (start us, length us, event | category | flops | bytes accessed | tf_op | source)
XLA Modules:
  0.0 218.6 jit_solution(11186598804903792471)
XLA Ops:
  8.3 5.1 %collective-permute-start.2 = (s32[4,64]{1,0:T(4,128)S(1)}, s32[4,64]{1,0:T(4,128)S(1)}, u32[]{:S(2)}, u32[]{:S(2)}) collective-permute-start(s32[4,64]{1,0:T(4,128)S(1)} %bitcast.112), channel_id=1, source_target_pairs={{0,12},{4,0},{8,4},{12,8},{1,13},{5,1},{9,5},{13,9},{2,14},{6,2},{... | collective-permute-start | bytes 3080 | tf_op jit(solution)/shard_map/ppermute | solution.py:47
  15.9 2.8 %collective-permute-start.29 = (bf16[64,2048]{1,0:T(8,128)(2,1)}, bf16[64,2048]{1,0:T(8,128)(2,1)}, u32[]{:S(2)}, u32[]{:S(2)}) collective-permute-start(bf16[64,2048]{1,0:T(8,128)(2,1)} %get-tuple-element.38), channel_id=1, source_target_pairs={{0,12},{4,0},{8,4},{12,8},{1,13},{5,1},{9,5},{13,9},{2,14},{6,2},{... | collective-permute-start | bytes 786440 | tf_op jit(solution)/shard_map/ppermute | solution.py:47
  22.3 3.8 %collective-permute-start.21 = (bf16[64,2048]{1,0:T(8,128)(2,1)}, bf16[64,2048]{1,0:T(8,128)(2,1)S(1)}, u32[]{:S(2)}, u32[]{:S(2)}) collective-permute-start(bf16[64,2048]{1,0:T(8,128)(2,1)} %get-tuple-element.30), channel_id=1, source_target_pairs={{0,12},{4,0},{8,4},{12,8},{1,13},{5,1},{9,5},{13,9},{2,14},{6,2},{... | collective-permute-start | bytes 786440 | tf_op jit(solution)/shard_map/ppermute | solution.py:47
  26.6 12.6 %collective-permute-start.19 = (bf16[64,2048]{1,0:T(8,128)(2,1)S(1)}, bf16[64,2048]{1,0:T(8,128)(2,1)S(1)}, u32[]{:S(2)}, u32[]{:S(2)}) collective-permute-start(bf16[64,2048]{1,0:T(8,128)(2,1)S(1)} %copy-done.1), channel_id=1, source_target_pairs={{0,4},{4,8},{8,12},{12,0},{1,5},{5,9},{9,13},{13,1},{2,6},{6,10},{... | collective-permute-start | bytes 786440 | tf_op jit(solution)/shard_map/ppermute | solution.py:47
  39.2 16.3 %collective-permute-done.28 = bf16[64,2048]{1,0:T(8,128)(2,1)} collective-permute-done((bf16[64,2048]{1,0:T(8,128)(2,1)}, bf16[64,2048]{1,0:T(8,128)(2,1)}, u32[]{:S(2)}, u32[]{:S(2)}) %collective-permute-start.28) | collective-permute-done | bytes 262176 | tf_op jit(solution)/shard_map/ppermute | solution.py:47
  55.5 8.7 %collective-permute-start.12 = (bf16[64,2048]{1,0:T(8,128)(2,1)S(1)}, bf16[64,2048]{1,0:T(8,128)(2,1)S(1)}, u32[]{:S(2)}, u32[]{:S(2)}) collective-permute-start(bf16[64,2048]{1,0:T(8,128)(2,1)S(1)} %get-tuple-element.23), channel_id=1, source_target_pairs={{0,8},{4,12},{8,0},{12,4},{1,9},{5,13},{9,1},{13,5},{2,10},{6,14},... | collective-permute-start | bytes 786440 | tf_op jit(solution)/shard_map/ppermute | solution.py:47
  64.2 6.2 %select_reduce_fusion = f32[256,64]{0,1:T(8,128)S(1)} fusion(bf16[32,2048,64]{1,2,0:T(8,128)(2,1)} %param.10, bf16[64,2048]{1,0:T(8,128)(2,1)} %collective-permute-done.29, bf16[64,2048]{1,0:T(8,128)(2,1)} %collective-permute-done.28, bf16[64,2048]{1,0:T(8,128)(2,1)} %collective-permute-done.27, bf16[64,2048]{1,0:T(8,128)(2,1)S(1)} %copy-done.2, ...), kind=kOutput, calls=%fused_computation.33 | convolution fusion | flops 2152710144 | bytes 9510912 | tf_op jit(solution)/shard_map/dot_general | solution.py:71
  70.4 4.7 %collective-permute-done.20 = bf16[64,2048]{1,0:T(8,128)(2,1)} collective-permute-done((bf16[64,2048]{1,0:T(8,128)(2,1)}, bf16[64,2048]{1,0:T(8,128)(2,1)}, u32[]{:S(2)}, u32[]{:S(2)}) %collective-permute-start.20) | collective-permute-done | bytes 262176 | tf_op jit(solution)/shard_map/ppermute | solution.py:47
  75.2 11.4 %collective-permute-start.4 = (bf16[64,2048]{1,0:T(8,128)(2,1)S(1)}, bf16[64,2048]{1,0:T(8,128)(2,1)S(1)}, u32[]{:S(2)}, u32[]{:S(2)}) collective-permute-start(bf16[64,2048]{1,0:T(8,128)(2,1)S(1)} %get-tuple-element.15), channel_id=1, source_target_pairs={{0,8},{4,12},{8,0},{12,4},{1,9},{5,13},{9,1},{13,5},{2,10},{6,14},... | collective-permute-start | bytes 786440 | tf_op jit(solution)/shard_map/ppermute | solution.py:47
  86.6 5.9 %select_reduce_fusion.1 = f32[256,64]{0,1:T(8,128)S(1)} fusion(bf16[32,2048,64]{1,2,0:T(8,128)(2,1)} %param.10, bf16[64,2048]{1,0:T(8,128)(2,1)S(1)} %collective-permute-done.21, bf16[64,2048]{1,0:T(8,128)(2,1)} %collective-permute-done.20, bf16[64,2048]{1,0:T(8,128)(2,1)S(1)} %collective-permute-done.19, bf16[64,2048]{1,0:T(8,128)(2,1)S(1)} %get-tuple-element.29, ...), kind=kOutput, calls=%fused_computation.34 | convolution fusion | flops 2152710144 | bytes 9510912 | tf_op jit(solution)/shard_map/dot_general | solution.py:71
  92.7 4.8 %collective-permute-done.12 = bf16[64,2048]{1,0:T(8,128)(2,1)S(1)} collective-permute-done((bf16[64,2048]{1,0:T(8,128)(2,1)S(1)}, bf16[64,2048]{1,0:T(8,128)(2,1)S(1)}, u32[]{:S(2)}, u32[]{:S(2)}) %collective-permute-start.12) | collective-permute-done | bytes 262176 | tf_op jit(solution)/shard_map/ppermute | solution.py:47
  98.0 2.5 %select_reduce_fusion.2 = f32[256,64]{0,1:T(8,128)S(1)} fusion(bf16[32,2048,64]{1,2,0:T(8,128)(2,1)S(1)} %bitcast.114, bf16[64,2048]{1,0:T(8,128)(2,1)S(1)} %collective-permute-done.13, bf16[64,2048]{1,0:T(8,128)(2,1)S(1)} %collective-permute-done.12, bf16[64,2048]{1,0:T(8,128)(2,1)S(1)} %collective-permute-done.11, ...), kind=kOutput, calls=%fused_computation.35 | convolution fusion | flops 2152710144 | bytes 9510912 | tf_op jit(solution)/shard_map/dot_general | solution.py:71
  100.7 8.8 %collective-permute-done.4 = bf16[64,2048]{1,0:T(8,128)(2,1)S(1)} collective-permute-done((bf16[64,2048]{1,0:T(8,128)(2,1)S(1)}, bf16[64,2048]{1,0:T(8,128)(2,1)S(1)}, u32[]{:S(2)}, u32[]{:S(2)}) %collective-permute-start.4) | collective-permute-done | bytes 262176 | tf_op jit(solution)/shard_map/ppermute | solution.py:47
  109.5 2.5 %select_reduce_fusion.3 = f32[256,64]{0,1:T(8,128)S(1)} fusion(bf16[32,2048,64]{1,2,0:T(8,128)(2,1)S(1)} %bitcast.114, bf16[64,2048]{1,0:T(8,128)(2,1)S(1)} %collective-permute-done.5, bf16[64,2048]{1,0:T(8,128)(2,1)S(1)} %collective-permute-done.4, bf16[64,2048]{1,0:T(8,128)(2,1)S(1)} %collective-permute-done.3, ...), kind=kOutput, calls=%fused_computation.36 | convolution fusion | flops 2152710144 | bytes 9510912 | tf_op jit(solution)/shard_map/dot_general | solution.py:71
  121.1 2.8 %collective-permute-start.32 = (bf16[64,2048]{1,0:T(8,128)(2,1)S(1)}, bf16[64,2048]{1,0:T(8,128)(2,1)}, u32[]{:S(2)}, u32[]{:S(2)}) collective-permute-start(bf16[64,2048]{1,0:T(8,128)(2,1)S(1)} %get-tuple-element.36), channel_id=1, source_target_pairs={{0,12},{4,0},{8,4},{12,8},{1,13},{5,1},{9,5},{13,9},{2,14},{6,2},{... | collective-permute-start | bytes 786440 | tf_op jit(solution)/shard_map/ppermute | solution.py:47
  128.6 2.4 %fusion.9 = bf16[256,2048]{1,0:T(8,128)(2,1)S(1)} fusion(bf16[32,64,2048]{2,1,0:T(8,128)(2,1)S(1)} %bitcast.116, pred[256,32]{0,1:T(8,128)(4,1)S(1)} %iota_compare_fusion.5, bf16[256,64]{0,1:T(8,128)(2,1)S(1)} %add_convert_fusion.2), kind=kOutput, calls=%fused_computation.17 | convolution fusion | flops 2148532224 | bytes 9478144 | tf_op jit(solution)/shard_map/dot_general | solution.py:76
  131.0 2.4 %fusion.8 = bf16[256,2048]{1,0:T(8,128)(2,1)S(1)} fusion(bf16[32,64,2048]{2,1,0:T(8,128)(2,1)S(1)} %bitcast.116, pred[256,32]{0,1:T(8,128)(4,1)S(1)} %iota_compare_fusion.6, bf16[256,64]{0,1:T(8,128)(2,1)S(1)} %add_convert_fusion.3), kind=kOutput, calls=%fused_computation.16 | convolution fusion | flops 2148532224 | bytes 9478144 | tf_op jit(solution)/shard_map/dot_general | solution.py:76
  133.5 3.0 %collective-permute-start.24 = (bf16[64,2048]{1,0:T(8,128)(2,1)S(1)}, bf16[64,2048]{1,0:T(8,128)(2,1)}, u32[]{:S(2)}, u32[]{:S(2)}) collective-permute-start(bf16[64,2048]{1,0:T(8,128)(2,1)S(1)} %get-tuple-element.28), channel_id=1, source_target_pairs={{0,12},{4,0},{8,4},{12,8},{1,13},{5,1},{9,5},{13,9},{2,14},{6,2},{... | collective-permute-start | bytes 786440 | tf_op jit(solution)/shard_map/ppermute | solution.py:47
  136.5 13.9 %collective-permute-done.33 = bf16[64,2048]{1,0:T(8,128)(2,1)S(1)} collective-permute-done((bf16[64,2048]{1,0:T(8,128)(2,1)S(1)}, bf16[64,2048]{1,0:T(8,128)(2,1)S(1)}, u32[]{:S(2)}, u32[]{:S(2)}) %collective-permute-start.33) | collective-permute-done | bytes 262176 | tf_op jit(solution)/shard_map/ppermute | solution.py:47
  151.1 5.9 %collective-permute-start.18 = (bf16[64,2048]{1,0:T(8,128)(2,1)S(1)}, bf16[64,2048]{1,0:T(8,128)(2,1)}, u32[]{:S(2)}, u32[]{:S(2)}) collective-permute-start(bf16[64,2048]{1,0:T(8,128)(2,1)S(1)} %get-tuple-element.18), channel_id=1, source_target_pairs={{0,4},{4,8},{8,12},{12,0},{1,5},{5,9},{9,13},{13,1},{2,6},{6,10},{... | collective-permute-start | bytes 786440 | tf_op jit(solution)/shard_map/ppermute | solution.py:47
  157.0 23.8 %fusion.130 = f32[512,2048]{1,0:T(8,128)S(1)} fusion(bf16[512,8192]{1,0:T(8,128)(2,1)} %all-gather.2.cloned.1.call-done, bf16[8192,2048]{1,0:T(8,128)(2,1)} %param.9), kind=kOutput, calls=%fused_computation.176 | convolution fusion | flops 17179869184 | bytes 46137344 | tf_op jit(solution)/shard_map/dot_general | solution.py:62
  180.9 3.6 %collective-permute-start.17 = (bf16[64,2048]{1,0:T(8,128)(2,1)S(1)}, bf16[64,2048]{1,0:T(8,128)(2,1)S(1)}, u32[]{:S(2)}, u32[]{:S(2)}) collective-permute-start(bf16[64,2048]{1,0:T(8,128)(2,1)S(1)} %get-tuple-element.19), channel_id=1, source_target_pairs={{0,8},{4,12},{8,0},{12,4},{1,9},{5,13},{9,1},{13,5},{2,10},{6,14},... | collective-permute-start | bytes 786440 | tf_op jit(solution)/shard_map/ppermute | solution.py:47
  191.8 8.0 %collective-permute-done.17 = bf16[64,2048]{1,0:T(8,128)(2,1)S(1)} collective-permute-done((bf16[64,2048]{1,0:T(8,128)(2,1)S(1)}, bf16[64,2048]{1,0:T(8,128)(2,1)S(1)}, u32[]{:S(2)}, u32[]{:S(2)}) %collective-permute-start.17) | collective-permute-done | bytes 262176 | tf_op jit(solution)/shard_map/ppermute | solution.py:47
  201.1 8.7 %collective-permute-done.9 = bf16[64,2048]{1,0:T(8,128)(2,1)S(1)} collective-permute-done((bf16[64,2048]{1,0:T(8,128)(2,1)S(1)}, bf16[64,2048]{1,0:T(8,128)(2,1)S(1)}, u32[]{:S(2)}, u32[]{:S(2)}) %collective-permute-start.9) | collective-permute-done | bytes 262176 | tf_op jit(solution)/shard_map/ppermute | solution.py:47
  (135 shorter events, 34.0 us)
Async XLA Ops:
  6.5 150.5 %all-gather.2.cloned.1.call-start = ((), (), s32[]{:S(2)}) async-start(), calls=%async_computation | async-start | bytes 10485760 | tf_op jit(solution)/shard_map/all_gather | solution.py:59
  18.7 36.8 %collective-permute-start.28 = (bf16[64,2048]{1,0:T(8,128)(2,1)}, bf16[64,2048]{1,0:T(8,128)(2,1)}, u32[]{:S(2)}, u32[]{:S(2)}) collective-permute-start(bf16[64,2048]{1,0:T(8,128)(2,1)} %get-tuple-element.39), channel_id=1, source_target_pairs={{0,8},{4,12},{8,0},{12,4},{1,9},{5,13},{9,1},{13,5},{2,10},{6,14},... | collective-permute-start | bytes 786440 | tf_op jit(solution)/shard_map/ppermute | solution.py:47
  22.2 33.3 %collective-permute-start.27 = (bf16[64,2048]{1,0:T(8,128)(2,1)}, bf16[64,2048]{1,0:T(8,128)(2,1)}, u32[]{:S(2)}, u32[]{:S(2)}) collective-permute-start(bf16[64,2048]{1,0:T(8,128)(2,1)} %get-tuple-element.40), channel_id=1, source_target_pairs={{0,4},{4,8},{8,12},{12,0},{1,5},{5,9},{9,13},{13,1},{2,6},{6,10},{... | collective-permute-start | bytes 786440 | tf_op jit(solution)/shard_map/ppermute | solution.py:47
  22.3 48.1 %collective-permute-start.21 = (bf16[64,2048]{1,0:T(8,128)(2,1)}, bf16[64,2048]{1,0:T(8,128)(2,1)S(1)}, u32[]{:S(2)}, u32[]{:S(2)}) collective-permute-start(bf16[64,2048]{1,0:T(8,128)(2,1)} %get-tuple-element.30), channel_id=1, source_target_pairs={{0,12},{4,0},{8,4},{12,8},{1,13},{5,1},{9,5},{13,9},{2,14},{6,2},{... | collective-permute-start | bytes 786440 | tf_op jit(solution)/shard_map/ppermute | solution.py:47
  26.1 49.0 %collective-permute-start.20 = (bf16[64,2048]{1,0:T(8,128)(2,1)}, bf16[64,2048]{1,0:T(8,128)(2,1)}, u32[]{:S(2)}, u32[]{:S(2)}) collective-permute-start(bf16[64,2048]{1,0:T(8,128)(2,1)} %get-tuple-element.31), channel_id=1, source_target_pairs={{0,8},{4,12},{8,0},{12,4},{1,9},{5,13},{9,1},{13,5},{2,10},{6,14},... | collective-permute-start | bytes 786440 | tf_op jit(solution)/shard_map/ppermute | solution.py:47
  26.6 48.6 %collective-permute-start.19 = (bf16[64,2048]{1,0:T(8,128)(2,1)S(1)}, bf16[64,2048]{1,0:T(8,128)(2,1)S(1)}, u32[]{:S(2)}, u32[]{:S(2)}) collective-permute-start(bf16[64,2048]{1,0:T(8,128)(2,1)S(1)} %copy-done.1), channel_id=1, source_target_pairs={{0,4},{4,8},{8,12},{12,0},{1,5},{5,9},{9,13},{13,1},{2,6},{6,10},{... | collective-permute-start | bytes 786440 | tf_op jit(solution)/shard_map/ppermute | solution.py:47
  55.5 37.0 %collective-permute-start.13 = (bf16[64,2048]{1,0:T(8,128)(2,1)S(1)}, bf16[64,2048]{1,0:T(8,128)(2,1)S(1)}, u32[]{:S(2)}, u32[]{:S(2)}) collective-permute-start(bf16[64,2048]{1,0:T(8,128)(2,1)S(1)} %get-tuple-element.22), channel_id=1, source_target_pairs={{0,12},{4,0},{8,4},{12,8},{1,13},{5,1},{9,5},{13,9},{2,14},{6,2},{... | collective-permute-start | bytes 786440 | tf_op jit(solution)/shard_map/ppermute | solution.py:47
  55.5 42.0 %collective-permute-start.12 = (bf16[64,2048]{1,0:T(8,128)(2,1)S(1)}, bf16[64,2048]{1,0:T(8,128)(2,1)S(1)}, u32[]{:S(2)}, u32[]{:S(2)}) collective-permute-start(bf16[64,2048]{1,0:T(8,128)(2,1)S(1)} %get-tuple-element.23), channel_id=1, source_target_pairs={{0,8},{4,12},{8,0},{12,4},{1,9},{5,13},{9,1},{13,5},{2,10},{6,14},... | collective-permute-start | bytes 786440 | tf_op jit(solution)/shard_map/ppermute | solution.py:47
  70.4 27.1 %collective-permute-start.11 = (bf16[64,2048]{1,0:T(8,128)(2,1)S(1)}, bf16[64,2048]{1,0:T(8,128)(2,1)S(1)}, u32[]{:S(2)}, u32[]{:S(2)}) collective-permute-start(bf16[64,2048]{1,0:T(8,128)(2,1)S(1)} %get-tuple-element.24), channel_id=1, source_target_pairs={{0,4},{4,8},{8,12},{12,0},{1,5},{5,9},{9,13},{13,1},{2,6},{6,10},{... | collective-permute-start | bytes 786440 | tf_op jit(solution)/shard_map/ppermute | solution.py:47
  75.2 25.4 %collective-permute-start.5 = (bf16[64,2048]{1,0:T(8,128)(2,1)S(1)}, bf16[64,2048]{1,0:T(8,128)(2,1)S(1)}, u32[]{:S(2)}, u32[]{:S(2)}) collective-permute-start(bf16[64,2048]{1,0:T(8,128)(2,1)S(1)} %get-tuple-element.14), channel_id=1, source_target_pairs={{0,12},{4,0},{8,4},{12,8},{1,13},{5,1},{9,5},{13,9},{2,14},{6,2},{... | collective-permute-start | bytes 786440 | tf_op jit(solution)/shard_map/ppermute | solution.py:47
  75.2 34.4 %collective-permute-start.4 = (bf16[64,2048]{1,0:T(8,128)(2,1)S(1)}, bf16[64,2048]{1,0:T(8,128)(2,1)S(1)}, u32[]{:S(2)}, u32[]{:S(2)}) collective-permute-start(bf16[64,2048]{1,0:T(8,128)(2,1)S(1)} %get-tuple-element.15), channel_id=1, source_target_pairs={{0,8},{4,12},{8,0},{12,4},{1,9},{5,13},{9,1},{13,5},{2,10},{6,14},... | collective-permute-start | bytes 786440 | tf_op jit(solution)/shard_map/ppermute | solution.py:47
  92.5 17.1 %collective-permute-start.3 = (bf16[64,2048]{1,0:T(8,128)(2,1)S(1)}, bf16[64,2048]{1,0:T(8,128)(2,1)S(1)}, u32[]{:S(2)}, u32[]{:S(2)}) collective-permute-start(bf16[64,2048]{1,0:T(8,128)(2,1)S(1)} %get-tuple-element.16), channel_id=1, source_target_pairs={{0,4},{4,8},{8,12},{12,0},{1,5},{5,9},{9,13},{13,1},{2,6},{6,10},{... | collective-permute-start | bytes 786440 | tf_op jit(solution)/shard_map/ppermute | solution.py:47
  97.5 16.2 %collective-permute-start.22 = (f32[256,64]{0,1:T(8,128)S(1)}, f32[256,64]{0,1:T(8,128)S(1)}, u32[]{:S(2)}, u32[]{:S(2)}) collective-permute-start(f32[256,64]{0,1:T(8,128)S(1)} %select_reduce_fusion.1), channel_id=1, source_target_pairs={{0,1},{1,0},{2,3},{3,2},{4,5},{5,4},{6,7},{7,6},{8,9},{9,8},{10,11... | collective-permute-start | bytes 196616 | tf_op jit(solution)/shard_map/ppermute | solution.py:22
  119.4 31.0 %collective-permute-start.33 = (bf16[64,2048]{1,0:T(8,128)(2,1)S(1)}, bf16[64,2048]{1,0:T(8,128)(2,1)S(1)}, u32[]{:S(2)}, u32[]{:S(2)}) collective-permute-start(bf16[64,2048]{1,0:T(8,128)(2,1)S(1)} %get-tuple-element.35), channel_id=1, source_target_pairs={{0,8},{4,12},{8,0},{12,4},{1,9},{5,13},{9,1},{13,5},{2,10},{6,14},... | collective-permute-start | bytes 786440 | tf_op jit(solution)/shard_map/ppermute | solution.py:47
  121.1 59.8 %collective-permute-start.32 = (bf16[64,2048]{1,0:T(8,128)(2,1)S(1)}, bf16[64,2048]{1,0:T(8,128)(2,1)}, u32[]{:S(2)}, u32[]{:S(2)}) collective-permute-start(bf16[64,2048]{1,0:T(8,128)(2,1)S(1)} %get-tuple-element.36), channel_id=1, source_target_pairs={{0,12},{4,0},{8,4},{12,8},{1,13},{5,1},{9,5},{13,9},{2,14},{6,2},{... | collective-permute-start | bytes 786440 | tf_op jit(solution)/shard_map/ppermute | solution.py:47
  127.1 57.3 %collective-permute-start.26 = (bf16[64,2048]{1,0:T(8,128)(2,1)}, bf16[64,2048]{1,0:T(8,128)(2,1)}, u32[]{:S(2)}, u32[]{:S(2)}) collective-permute-start(bf16[64,2048]{1,0:T(8,128)(2,1)} %get-tuple-element.26), channel_id=1, source_target_pairs={{0,4},{4,8},{8,12},{12,0},{1,5},{5,9},{9,13},{13,1},{2,6},{6,10},{... | collective-permute-start | bytes 786440 | tf_op jit(solution)/shard_map/ppermute | solution.py:47
  127.1 58.6 %collective-permute-start.25 = (bf16[64,2048]{1,0:T(8,128)(2,1)S(1)}, bf16[64,2048]{1,0:T(8,128)(2,1)}, u32[]{:S(2)}, u32[]{:S(2)}) collective-permute-start(bf16[64,2048]{1,0:T(8,128)(2,1)S(1)} %get-tuple-element.27), channel_id=1, source_target_pairs={{0,8},{4,12},{8,0},{12,4},{1,9},{5,13},{9,1},{13,5},{2,10},{6,14},... | collective-permute-start | bytes 786440 | tf_op jit(solution)/shard_map/ppermute | solution.py:47
  133.5 54.3 %collective-permute-start.24 = (bf16[64,2048]{1,0:T(8,128)(2,1)S(1)}, bf16[64,2048]{1,0:T(8,128)(2,1)}, u32[]{:S(2)}, u32[]{:S(2)}) collective-permute-start(bf16[64,2048]{1,0:T(8,128)(2,1)S(1)} %get-tuple-element.28), channel_id=1, source_target_pairs={{0,12},{4,0},{8,4},{12,8},{1,13},{5,1},{9,5},{13,9},{2,14},{6,2},{... | collective-permute-start | bytes 786440 | tf_op jit(solution)/shard_map/ppermute | solution.py:47
  151.1 36.8 %collective-permute-start.18 = (bf16[64,2048]{1,0:T(8,128)(2,1)S(1)}, bf16[64,2048]{1,0:T(8,128)(2,1)}, u32[]{:S(2)}, u32[]{:S(2)}) collective-permute-start(bf16[64,2048]{1,0:T(8,128)(2,1)S(1)} %get-tuple-element.18), channel_id=1, source_target_pairs={{0,4},{4,8},{8,12},{12,0},{1,5},{5,9},{9,13},{13,1},{2,6},{6,10},{... | collective-permute-start | bytes 786440 | tf_op jit(solution)/shard_map/ppermute | solution.py:47
  180.9 18.9 %collective-permute-start.17 = (bf16[64,2048]{1,0:T(8,128)(2,1)S(1)}, bf16[64,2048]{1,0:T(8,128)(2,1)S(1)}, u32[]{:S(2)}, u32[]{:S(2)}) collective-permute-start(bf16[64,2048]{1,0:T(8,128)(2,1)S(1)} %get-tuple-element.19), channel_id=1, source_target_pairs={{0,8},{4,12},{8,0},{12,4},{1,9},{5,13},{9,1},{13,5},{2,10},{6,14},... | collective-permute-start | bytes 786440 | tf_op jit(solution)/shard_map/ppermute | solution.py:47
  184.4 15.3 %collective-permute-start.16 = (bf16[64,2048]{1,0:T(8,128)(2,1)S(1)}, bf16[64,2048]{1,0:T(8,128)(2,1)S(1)}, u32[]{:S(2)}, u32[]{:S(2)}) collective-permute-start(bf16[64,2048]{1,0:T(8,128)(2,1)S(1)} %get-tuple-element.20), channel_id=1, source_target_pairs={{0,12},{4,0},{8,4},{12,8},{1,13},{5,1},{9,5},{13,9},{2,14},{6,2},{... | collective-permute-start | bytes 786440 | tf_op jit(solution)/shard_map/ppermute | solution.py:47
  185.8 15.3 %collective-permute-start.10 = (bf16[64,2048]{1,0:T(8,128)(2,1)S(1)}, bf16[64,2048]{1,0:T(8,128)(2,1)S(1)}, u32[]{:S(2)}, u32[]{:S(2)}) collective-permute-start(bf16[64,2048]{1,0:T(8,128)(2,1)S(1)} %get-tuple-element.10), channel_id=1, source_target_pairs={{0,4},{4,8},{8,12},{12,0},{1,5},{5,9},{9,13},{13,1},{2,6},{6,10},{... | collective-permute-start | bytes 786440 | tf_op jit(solution)/shard_map/ppermute | solution.py:47
  187.8 22.0 %collective-permute-start.9 = (bf16[64,2048]{1,0:T(8,128)(2,1)S(1)}, bf16[64,2048]{1,0:T(8,128)(2,1)S(1)}, u32[]{:S(2)}, u32[]{:S(2)}) collective-permute-start(bf16[64,2048]{1,0:T(8,128)(2,1)S(1)} %get-tuple-element.11), channel_id=1, source_target_pairs={{0,8},{4,12},{8,0},{12,4},{1,9},{5,13},{9,1},{13,5},{2,10},{6,14},... | collective-permute-start | bytes 786440 | tf_op jit(solution)/shard_map/ppermute | solution.py:47
  187.9 21.9 %collective-permute-start.8 = (bf16[64,2048]{1,0:T(8,128)(2,1)S(1)}, bf16[64,2048]{1,0:T(8,128)(2,1)S(1)}, u32[]{:S(2)}, u32[]{:S(2)}) collective-permute-start(bf16[64,2048]{1,0:T(8,128)(2,1)S(1)} %get-tuple-element.12), channel_id=1, source_target_pairs={{0,12},{4,0},{8,4},{12,8},{1,13},{5,1},{9,5},{13,9},{2,14},{6,2},{... | collective-permute-start | bytes 786440 | tf_op jit(solution)/shard_map/ppermute | solution.py:47
  (27 other events, 391.4 us)
Sparse Core Ops, SparseCore 0:
  8.9 60.9 all-gather.1

commit v3 on v2

v3 whole, which is shorter than its diff:
```python
import functools

import jax
import jax.numpy as jnp
from jax import lax
from jax.experimental import pallas as pl
from jax.experimental.pallas import tpu as pltpu
from jax.sharding import PartitionSpec as P


def row_places(slots, adp_dev):
    row_count = slots.shape[-1]
    owner = slots // adp_dev
    index = jnp.arange(row_count, dtype=jnp.int32)
    before = index[None, :] < index[:, None]
    same = owner[..., :, None] == owner[..., None, :]
    place = jnp.sum((same & before).astype(jnp.int32), axis=-1)
    return owner, place


MESH = pl.DeviceIdType.MESH
LANES = 128
TILE = 512


def kernel(
    groups, shards, send_ref, act_ref, mark_ref, wide_ref, back_ref, base_ref, down_ref, up_ref,
    out_ref, rows, acts, total, down, up, delta, back, part, parts, tiles,
    row_send, row_recv, act_send, act_recv, part_send, part_recv, back_send, back_recv, load, stream,
):
    steps, count, width = rows.shape
    capacity = count // groups
    columns = up_ref.shape[1]
    inner = up_ref.shape[0]
    me_ad, me_tp = lax.axis_index("ad"), lax.axis_index("tp")

    def on_ad(k):
        return {"ad": lax.rem(me_ad + k + groups, groups)}

    def on_tp(k):
        return {"tp": lax.rem(me_tp + k, shards)}

    def block(k):
        return pl.ds(k * capacity, capacity)

    def remote(src, dst, send_sem, recv_sem, device):
        return pltpu.make_async_remote_copy(
            src_ref=src, dst_ref=dst, send_sem=send_sem, recv_sem=recv_sem,
            device_id=device, device_id_type=MESH,
        )

    def row_copy(s, k):
        return remote(send_ref.at[s, k], rows.at[s, block(k)], row_send.at[s, k],
                      row_recv.at[s, k], on_ad(k))

    def act_copy(k):
        return remote(act_ref, acts.at[k], act_send.at[k], act_recv.at[k], on_tp(k))

    def part_copy(s, k):
        return remote(part.at[s], parts.at[s, k], part_send.at[s, k], part_recv.at[s, k], on_tp(k))

    def back_copy(s, k):
        return remote(delta.at[s, block(k)], back.at[s, block(k)], back_send.at[s, k],
                      back_recv.at[s, k], on_ad(-k))

    barrier = pltpu.get_barrier_semaphore()
    for k in range(1, groups):
        pl.semaphore_signal(barrier, inc=1, device_id=on_ad(k), device_id_type=MESH)
    for k in range(1, shards):
        pl.semaphore_signal(barrier, inc=1, device_id=on_tp(k), device_id_type=MESH)
    pl.semaphore_wait(barrier, groups + shards - 2)

    for s in range(steps):
        for k in range(1, groups):
            row_copy(s, k).start()
    for k in range(1, shards):
        act_copy(k).start()
    own = [pltpu.make_async_copy(send_ref.at[s, 0], rows.at[s, block(0)], load.at[3 + s])
           for s in range(steps)]
    loads = [
        pltpu.make_async_copy(act_ref, acts.at[0], load.at[0]),
        pltpu.make_async_copy(down_ref, down, load.at[1]),
        pltpu.make_async_copy(up_ref, up, load.at[2]),
    ]
    for copy in loads + own:
        copy.start()

    step_columns = tiles.shape[2]
    per_shard = columns // step_columns

    def add_base(k):
        source = lax.rem(me_tp - k + shards, shards)

        def tile_copy(n):
            return pltpu.make_async_copy(
                base_ref.at[pl.ds(source * width, width), pl.ds(n * step_columns, step_columns)],
                tiles.at[n % 2], stream.at[n % 2],
            )

        tile_copy(0).start()
        for n in range(per_shard):
            if n + 1 < per_shard:
                tile_copy(n + 1).start()
            tile_copy(n).wait()
            where = pl.ds(n * step_columns, step_columns)

            @pl.loop(0, steps)
            def _(s):
                piece = pl.ds(s * row_count, row_count)
                value = jnp.dot(
                    acts[k, piece, :], tiles[n % 2], preferred_element_type=jnp.float32
                )
                if k == 0:
                    total[piece, where] = value
                else:
                    total[piece, where] += value

    row_count = out_ref.shape[1]
    loads[0].wait()
    add_base(0)
    loads[1].wait()

    def shrink(s):
        own[s].wait()
        for k in range(1, groups):
            row_copy(s, k).wait_recv()
        part[s] = jnp.zeros((count, LANES), jnp.float32)

        @pl.loop(0, inner // TILE)
        def _(n):
            where = pl.ds(pl.multiple_of(n * TILE, TILE), TILE)
            every = lax.dot_general(
                rows[s], down[where, :], (((1,), (1,)), ((), ())),
                preferred_element_type=jnp.float32,
            )
            mask = jnp.dot(mark_ref[s], wide_ref[:, where], preferred_element_type=jnp.float32)
            every = jnp.where(mask > 0.5, every, 0.0)
            value = part[s]
            for j in range(TILE // LANES):
                value += every[:, j * LANES:(j + 1) * LANES]
            part[s] = value

        for k in range(1, shards):
            part_copy(s, k).start()

    def expand(s):
        low = part[s]
        for k in range(1, shards):
            part_copy(s, k).wait_recv()
            low += parts[s, k]
        low = low + pltpu.roll(low, LANES // 2, 1)
        low = low.astype(jnp.bfloat16).astype(jnp.float32)
        low = jnp.concatenate([low] * (inner // LANES), axis=1)
        mask = jnp.dot(mark_ref[s], wide_ref[...], preferred_element_type=jnp.float32)
        spread = jnp.where(mask > 0.5, low, 0.0).astype(jnp.bfloat16)
        for n in range(columns // step_columns):
            where = pl.ds(n * step_columns, step_columns)
            value = jnp.dot(
                spread, up[:, where], preferred_element_type=jnp.float32
            ).astype(jnp.bfloat16)
            delta[s, :, where] = value
            back[s, block(0), where] = value[:capacity]
        for k in range(1, groups):
            back_copy(s, k).start()

    for s in range(steps):
        shrink(s)
        if s == 1:
            loads[2].wait()
        if s >= 1:
            expand(s - 1)
    expand(steps - 1)

    for k in range(1, shards):
        act_copy(k).wait_recv()
        add_base(k)

    for s in range(steps):
        for k in range(1, groups):
            back_copy(s, k).wait_recv()
        for n in range(columns // step_columns):
            where = pl.ds(n * step_columns, step_columns)
            value = jnp.dot(back_ref[s], back[s, :, where], preferred_element_type=jnp.float32)
            value += total[pl.ds(s * row_count, row_count), where]
            out_ref[s, :, where] = value.astype(jnp.bfloat16)

    for s in range(steps):
        for k in range(1, groups):
            row_copy(s, k).wait_send()
            back_copy(s, k).wait_send()
        for k in range(1, shards):
            part_copy(s, k).wait_send()
    for k in range(1, shards):
        act_copy(k).wait_send()


def body(activations, adapter_ids, owner_slots, base_weight, shrink_weight, expand_weight):
    steps, row_count, width = activations.shape
    adp_dev, _, rank = shrink_weight.shape
    columns = base_weight.shape[1]
    groups = lax.axis_size("ad")
    me = lax.axis_index("ad")
    capacity = row_count // 2

    matches = adapter_ids[..., None] == jnp.arange(owner_slots.shape[0], dtype=jnp.int32)
    slots = jnp.sum(jnp.where(matches, owner_slots, 0), axis=-1)
    owner, place = row_places(slots, adp_dev)
    target = lax.rem(owner - me + groups, groups) * capacity + place
    hit = target[:, None, :] == jnp.arange(groups * capacity, dtype=jnp.int32)[None, :, None]
    places = hit.astype(jnp.bfloat16)
    marks = jnp.sum(jnp.where(hit, (slots % adp_dev + 1)[:, None, :], 0), axis=-1) - 1
    marks = marks.reshape(steps, groups, capacity)

    def shifted(block, k):
        if k % groups == 0:
            return block
        return lax.ppermute(block, "ad", [(i, (i + k) % groups) for i in range(groups)])

    local = jnp.stack([shifted(marks[:, k], k) for k in range(groups)], axis=1)

    send = jnp.einsum(
        "scr,srf->scf", places, activations, preferred_element_type=jnp.float32
    ).astype(jnp.bfloat16).reshape(steps, groups, capacity, width)
    shards = lax.axis_size("tp")
    count = groups * capacity
    inner = adp_dev * rank
    adapter = jnp.arange(adp_dev, dtype=jnp.int32)
    mark = (local.reshape(steps, count, 1) == adapter).astype(jnp.bfloat16)
    wide = (adapter[:, None] == jnp.arange(inner, dtype=jnp.int32) // rank).astype(jnp.bfloat16)
    anywhere = pl.BlockSpec(memory_space=pl.ANY)
    vmem = pl.BlockSpec(memory_space=pltpu.VMEM)
    dma = pltpu.SemaphoreType.DMA
    tile_columns = min(TILE, columns)
    return pl.pallas_call(
        functools.partial(kernel, groups, shards),
        out_shape=jax.ShapeDtypeStruct((steps, row_count, columns), jnp.bfloat16),
        in_specs=[anywhere, anywhere, vmem, vmem, vmem, anywhere, anywhere, anywhere],
        out_specs=vmem,
        scratch_shapes=[
            pltpu.VMEM((steps, count, width), jnp.bfloat16),
            pltpu.VMEM((shards, steps * row_count, width), jnp.bfloat16),
            pltpu.VMEM((steps * row_count, columns), jnp.float32),
            pltpu.VMEM((inner, width), jnp.bfloat16),
            pltpu.VMEM((inner, columns), jnp.bfloat16),
            pltpu.VMEM((steps, count, columns), jnp.bfloat16),
            pltpu.VMEM((steps, count, columns), jnp.bfloat16),
            pltpu.VMEM((steps, count, LANES), jnp.float32),
            pltpu.VMEM((steps, shards, count, LANES), jnp.float32),
            pltpu.VMEM((2, width, tile_columns), jnp.bfloat16),
            dma((steps, groups)),
            dma((steps, groups)),
            dma((shards,)),
            dma((shards,)),
            dma((steps, shards)),
            dma((steps, shards)),
            dma((steps, groups)),
            dma((steps, groups)),
            dma((3 + steps,)),
            dma((2,)),
        ],
        compiler_params=pltpu.CompilerParams(
            collective_id=0, has_side_effects=True, vmem_limit_bytes=60 * 1024 * 1024
        ),
        cost_estimate=pl.CostEstimate(
            flops=2 * steps * (row_count * shards + 2 * count) * inner * width,
            bytes_accessed=2 * (shards * width * columns + 2 * inner * width),
            transcendentals=0,
        ),
    )(
        send,
        activations.reshape(steps * row_count, width),
        mark,
        wide,
        places.transpose(0, 2, 1),
        base_weight,
        shrink_weight.transpose(0, 2, 1).reshape(inner, width),
        expand_weight.reshape(inner, columns),
    )


def solution(mesh):
    in_specs = (
        P(None, ("rep", "ad"), "tp"),
        P(None, ("rep", "ad")),
        P("rep"),
        P(None, "tp"),
        P(("rep", "ad"), "tp", None),
        P(("rep", "ad"), None, "tp"),
    )
    out_specs = P(None, ("rep", "ad"), "tp")
    return jax.shard_map(body, mesh=mesh, in_specs=in_specs, out_specs=out_specs, check_vma=False)
```

time: 219 us -> 215 us (0.982)
  Pallas kernels: 0 us -> 195 us
  starting transfers between devices: 74.8 us -> 6.11 us
  waiting for transfers between devices: 66.3 us -> 0.01 us
  matrix products: 56.6 us -> 4.75 us
  between operations: 13.9 us -> 0.06 us
    pallas_call x0 -> x1, Pallas kernels: none -> 195 us  [body(): pl.pallas_call(functools.partial(kernel, groups, shards), out_shape=jax.S...]
    ppermute x27 -> x3, waiting for transfers between devices: 65.3 us -> 0.01 us  [shifted(): lax.ppermute(block, 'ad', [(i, (i + k) % groups) for i in range(groups)])]
    ppermute x27 -> x3, starting transfers between devices: 69.8 us -> 6.11 us  [shifted(): lax.ppermute(block, 'ad', [(i, (i + k) % groups) for i in range(groups)])]
    dot_general x17 -> x1, matrix products: 56.6 us -> 4.75 us  [body(): jnp.einsum('scr,srf->scf', places, activations, preferred_element_type=jn...]
    ppermute x8 -> x0, starting transfers between devices: 4.99 us -> none  [sum_over_tp(): value = value + lax.ppermute(value, 'tp', pairs)]
    slice x9 -> x0, local copies, waits for them, and re-layouts: 3.09 us -> none  [the longest x4 2.04 us: body(): send[k]]
    convert_element_type x4 -> x3, other arithmetic: 0.04 us -> 2.43 us  [the longest x1 0.91 us: body(): mark = (local.reshape(steps, count, 1) == adapter).astype(jnp.bfloat16)]
    unnamed x30 -> x1, local copies, waits for them, and re-layouts: 0.85 us -> 3.16 us
  transfers between devices with their start and end apart: 36 -> 3, of which waited for: 8 -> 0; matrix products, arithmetic and copies ran while one was open for 28% -> 3% of each run, Pallas kernels for 0% -> 0%
where the time goes in v3:
time: 215 us; the launch traced here: 213 us
  Pallas kernels  195 us (91%)
  starting transfers between devices  6.11 us (3%)
  matrix products  4.75 us (2%)
  other arithmetic  3.93 us (2%)
  local copies, waits for them, and re-layouts  3.34 us (2%)
    pallas_call x1, Pallas kernels, body(): pl.pallas_call(functools.partial(kernel, groups, shards), out_shape=jax.S...  195 us
    ppermute x3, starting transfers between devices, shifted(): lax.ppermute(block, 'ad', [(i, (i + k) % groups) for i in range(groups)])  6.11 us
    dot_general x1, matrix products, body(): jnp.einsum('scr,srf->scf', places, activations, preferred_element_type=jn...  4.75 us
  transfers between devices with their start and end apart: 3, of which 0 were waited for; matrix products, arithmetic and copies ran while one was open for 3% of the time, Pallas kernels for 0%

profile of v3, /device:TPU:0, one launch (start us, length us, event | category | flops | bytes accessed | tf_op | source)
XLA Modules:
  0.0 212.8 jit_solution(16513168798625904257)
XLA Ops:
  0.0 0.9 select_reduce_fusion.1
  1.0 0.2 convert_reduce_fusion
  1.2 0.3 select_reduce_fusion
  1.5 0.1 sub.32
  1.6 3.1 %collective-permute-start = (s32[4,64]{1,0:T(4,128)S(1)}, s32[4,64]{1,0:T(4,128)S(1)}, u32[]{:S(2)}, u32[]{:S(2)}) collective-permute-start(s32[4,64]{1,0:T(4,128)S(1)} %bitcast.25), channel_id=1, source_target_pairs={{0,4},{4,8},{8,12},{12,0},{1,5},{5,9},{9,13},{13,1},{2,6},{6,10},{... | collective-permute-start | bytes 3080 | tf_op jit(solution)/shard_map/ppermute | solution.py:217
  4.7 2.1 collective-permute-start.2
  6.8 0.9 collective-permute-start.1
  7.7 0.7 fusion.3.wide_ref
  8.4 4.8 %convolution_convert_fusion = bf16[4,256,2048]{2,1,0:T(8,128)(2,1)} fusion(bf16[4,128,2048]{2,1,0:T(8,128)(2,1)} %param.6, s32[4,128]{1,0:T(4,128)S(1)} %fusion.9), kind=kOutput, calls=%fused_computation | convolution fusion | flops 539099136 | bytes 6293504 | tf_op jit(solution)/shard_map/scr,srf->scf/dot_general | solution.py:221
  13.2 0.8 fusion.1.back_ref
  14.0 0.0 collective-permute-done
  14.0 0.0 collective-permute-done.2
  14.0 0.0 collective-permute-done.1
  14.1 0.1 eq.85
  14.1 0.9 fusion.mark_ref
  15.0 194.6 %shard_map.64 = bf16[4,128,2048]{2,1,0:T(8,128)(2,1)} custom-call(bf16[4,4,64,2048]{3,2,1,0:T(8,128)(2,1)} %bitcast.18, bf16[512,2048]{1,0:T(8,128)(2,1)} %bitcast.19, bf16[4,256,32]{2,1,0:T(8,128)(2,1)} %fusion.mark_ref, bf16[32,2048]{1,0:T(8,128)(2,1)} %fusion.3.wide_ref, bf16[4,128,256]{2,1,0:T(8,128)(2,1)} %fusion.1.back_ref, ...), custom_call_target="tpu_custom_call" | custom-call | flops 34359738368 | bytes 50331648 | tf_op jit(solution)/shard_map/pallas_call | solution.py:234
  209.6 3.2 %copy.25 = bf16[4,128,2048]{2,1,0:T(8,128)(2,1)} copy(bf16[4,128,2048]{2,1,0:T(8,128)(2,1)} %shard_map.64) | data formatting | bytes 4194304
  (8 shorter events, 0.1 us)
Async XLA Ops:
  1.6 12.4 %collective-permute-start = (s32[4,64]{1,0:T(4,128)S(1)}, s32[4,64]{1,0:T(4,128)S(1)}, u32[]{:S(2)}, u32[]{:S(2)}) collective-permute-start(s32[4,64]{1,0:T(4,128)S(1)} %bitcast.25), channel_id=1, source_target_pairs={{0,4},{4,8},{8,12},{12,0},{1,5},{5,9},{9,13},{13,1},{2,6},{6,10},{... | collective-permute-start | bytes 3080 | tf_op jit(solution)/shard_map/ppermute | solution.py:217
  4.7 9.3 %collective-permute-start.2 = (s32[4,64]{1,0:T(4,128)S(1)}, s32[4,64]{1,0:T(4,128)S(1)}, u32[]{:S(2)}, u32[]{:S(2)}) collective-permute-start(s32[4,64]{1,0:T(4,128)S(1)} %bitcast.23), channel_id=1, source_target_pairs={{0,12},{4,0},{8,4},{12,8},{1,13},{5,1},{9,5},{13,9},{2,14},{6,2},{... | collective-permute-start | bytes 3080 | tf_op jit(solution)/shard_map/ppermute | solution.py:217
  6.8 7.2 %collective-permute-start.1 = (s32[4,64]{1,0:T(4,128)S(1)}, s32[4,64]{1,0:T(4,128)S(1)}, u32[]{:S(2)}, u32[]{:S(2)}) collective-permute-start(s32[4,64]{1,0:T(4,128)S(1)} %bitcast.21), channel_id=1, source_target_pairs={{0,8},{4,12},{8,0},{12,4},{1,9},{5,13},{9,1},{13,5},{2,10},{6,14},... | collective-permute-start | bytes 3080 | tf_op jit(solution)/shard_map/ppermute | solution.py:217
